TPU v7x, 32 devices: a whole 2x2x4 slice. The times are simulated.
32 devices in a mesh: dp: 16 (over z, y, x), seq: 2 (over core).
Axes of the slice: x: 2, y: 2, z: 4, core: 2. Of those that a mesh axis runs over, the one named last changes fastest.
Arguments:
- latents: bfloat16 [16, 1024, 1152], P('dp', 'seq'), may hold values from -6 to 6
- condition: bfloat16 [16, 1152], P('dp'), may hold values from -6 to 6
- cotangent: bfloat16 [16, 1024, 1152], P('dp', 'seq'), may hold values from -6 to 6
- teacher: bfloat16 [16, 1024, 1152], P('dp', 'seq'), may hold values from -6 to 6
- valid_mask: int32 [16, 1024], P('dp', 'seq'), may hold values from 0 to 1, as said below
- modulation_weight: float32 [1152, 6912], P('seq', 'dp'), may hold values from -0.1875 to 0.1875
- attention_weight: float32 [1152, 3456], P('seq', 'dp'), may hold values from -0.1875 to 0.1875
- projection_weight: float32 [1152, 1152], P('seq', 'dp'), may hold values from -0.5 to 0.5
- expansion_weight: float32 [1152, 4608], P('seq', 'dp'), may hold values from -0.1875 to 0.1875
- contraction_weight: float32 [4608, 1152], P('seq', 'dp'), may hold values from -0.125 to 0.125
- modulation_moment: float32 [1152, 6912], P('seq', 'dp'), may hold values from -224 to 224
- attention_moment: float32 [1152, 3456], P('seq', 'dp'), may hold values from -80 to 80
- projection_moment: float32 [1152, 1152], P('seq', 'dp'), may hold values from -160 to 160
- expansion_moment: float32 [1152, 4608], P('seq', 'dp'), may hold values from -224 to 224
- contraction_moment: float32 [4608, 1152], P('seq', 'dp'), may hold values from -320 to 320
- modulation_average: float32 [1152, 6912], P('seq', 'dp'), may hold values from -0.1875 to 0.1875
- attention_average: float32 [1152, 3456], P('seq', 'dp'), may hold values from -0.1875 to 0.1875
- projection_average: float32 [1152, 1152], P('seq', 'dp'), may hold values from -0.5 to 0.5
- expansion_average: float32 [1152, 4608], P('seq', 'dp'), may hold values from -0.1875 to 0.1875
- contraction_average: float32 [4608, 1152], P('seq', 'dp'), may hold values from -0.125 to 0.125
Outputs:
- block_output: float32 [16, 1024, 1152], P('dp', 'seq')
- masked_loss: float32 [], replicated
- latent_grad: float32 [16, 1024, 1152], P('dp', 'seq')
- condition_grad: float32 [16, 1152], P('dp')
- modulation_next: float32 [1152, 6912], P('seq', 'dp')
- attention_next: float32 [1152, 3456], P('seq', 'dp')
- projection_next: float32 [1152, 1152], P('seq', 'dp')
- expansion_next: float32 [1152, 4608], P('seq', 'dp')
- contraction_next: float32 [4608, 1152], P('seq', 'dp')
- modulation_moment_next: float32 [1152, 6912], P('seq', 'dp')
- attention_moment_next: float32 [1152, 3456], P('seq', 'dp')
- projection_moment_next: float32 [1152, 1152], P('seq', 'dp')
- expansion_moment_next: float32 [1152, 4608], P('seq', 'dp')
- contraction_moment_next: float32 [4608, 1152], P('seq', 'dp')
- modulation_average_next: float32 [1152, 6912], P('seq', 'dp')
- attention_average_next: float32 [1152, 3456], P('seq', 'dp')
- projection_average_next: float32 [1152, 1152], P('seq', 'dp')
- expansion_average_next: float32 [1152, 4608], P('seq', 'dp')
- contraction_average_next: float32 [4608, 1152], P('seq', 'dp')
Inputs may be any that keep to these rules, and one draw needn't show every extreme that they name: `valid_mask`: the first token of every latent is valid.
All inputs are finite; a program needn't handle non-finite values.
Results may differ from a plain program's by a relative error of at most 0.02.
The roundings to bfloat16 on the way count: a program that leaves them out, or rounds other values in their place, can miss the bound.
Values may be sent and summed in bfloat16 or wider, within the bound.
No kernel may reach another device: no remote copies, remote signals or barrier semaphores. Data moves between devices by JAX's collectives and lax.ppermute only.
A program may use at most 320 MiB of HBM per device.

v0:
```python
import math

import jax
import jax.numpy as jnp
from jax import lax
from jax.sharding import PartitionSpec as P

HEADS = 16
SEQ_LEN = 1024


epsilon = 1e-06


def for_sending(array):

    def short(part):
        return part.astype(jnp.bfloat16) if part.dtype == jnp.float32 else part

    return jax.tree.map(short, array)


def silu_of(values):
    return values * jax.nn.sigmoid(values)


def gelu_of(values):
    tanh_input = 0.7978845608028654 * (values + 0.044715 * values * values * values)
    return 0.5 * values * (1.0 + jnp.tanh(tanh_input))


def modulated(values, offset, stretch):
    centered = values - jnp.mean(values, axis=-1, keepdims=True)
    variance = jnp.mean(centered * centered, axis=-1, keepdims=True)
    return centered * lax.rsqrt(variance + epsilon) * (1.0 + stretch) + offset


def project(first_matrix, second_matrix):
    return jnp.dot(first_matrix, second_matrix, preferred_element_type=jnp.float32)


def left_contract(first_matrix, second_matrix):
    return lax.dot_general(
        first_matrix, second_matrix, (((0,), (0,)), ((), ())), preferred_element_type=jnp.float32
    )


def right_contract(first_matrix, second_matrix):
    return lax.dot_general(
        first_matrix, second_matrix, (((1,), (1,)), ((), ())), preferred_element_type=jnp.float32
    )


def gather_weights(shards):
    row_full = jax.tree.map(
        lambda part, own: part.astype(own.dtype),
        lax.all_gather(for_sending(shards), "seq", axis=0, tiled=True),
        shards,
    )
    return jax.tree.map(
        lambda part, own: part.astype(own.dtype),
        lax.all_gather(for_sending(row_full), "dp", axis=1, tiled=True),
        row_full,
    )


def body(
    latents,
    condition,
    cotangent,
    teacher,
    valid_mask,
    modulation_weight,
    attention_weight,
    projection_weight,
    expansion_weight,
    contraction_weight,
    modulation_moment,
    attention_moment,
    projection_moment,
    expansion_moment,
    contraction_moment,
    modulation_average,
    attention_average,
    projection_average,
    expansion_average,
    contraction_average,
):
    local_latents, block_rows, model_width = latents.shape
    head_count = HEADS
    head_size = model_width // head_count
    score_scale = head_size ** (-0.5)
    tokens = local_latents * block_rows
    seq_devices = lax.axis_size("seq")
    masters = (
        modulation_weight,
        attention_weight,
        projection_weight,
        expansion_weight,
        contraction_weight,
    )
    low_shards = tuple((master.astype(jnp.bfloat16) for master in masters))
    mask_float = valid_mask.astype(jnp.float32)
    count_total = lax.psum(jnp.sum(mask_float), ("dp", "seq"))
    full_modulation, full_attention, full_projection, full_expansion, full_contraction = (
        gather_weights(low_shards)
    )
    residual_in = latents.astype(jnp.float32)
    cond_values = condition.astype(jnp.float32)
    silu_value, silu_pull = jax.vjp(silu_of, cond_values)
    cond_active = silu_value.astype(jnp.bfloat16)
    modulation = project(cond_active, full_modulation)
    shift_attn, scale_attn, gate_attn, shift_mlp, scale_mlp, gate_mlp = [
        column_group[:, None, :] for column_group in jnp.split(modulation, 6, axis=-1)
    ]
    attn_value, attn_pull = jax.vjp(modulated, residual_in, shift_attn, scale_attn)
    attn_input = attn_value.astype(jnp.bfloat16).reshape(tokens, model_width)
    qkv_values = (
        project(attn_input, full_attention)
        .astype(jnp.bfloat16)
        .reshape(local_latents, block_rows, 3 * model_width)
    )
    query_low = qkv_values[..., :model_width]
    key_low = qkv_values[..., model_width : 2 * model_width]
    value_low = qkv_values[..., 2 * model_width :]
    query_heads = query_low.reshape(local_latents, block_rows, head_count, head_size)
    running_max = jnp.full((local_latents, head_count, block_rows), -1e30, jnp.float32)
    key_piece = lax.all_gather(key_low, "seq", axis=1, tiled=True)
    value_piece = lax.all_gather(value_low, "seq", axis=1, tiled=True)
    span = key_piece.shape[1]
    key_heads = key_piece.reshape(local_latents, span, head_count, head_size)
    value_heads = value_piece.reshape(local_latents, span, head_count, head_size)
    scores = (
        jnp.einsum("lqhd,lkhd->lhqk", query_heads, key_heads, preferred_element_type=jnp.float32)
        * score_scale
    )
    newest_max = jnp.maximum(running_max, jnp.max(scores, axis=-1))
    raised = jnp.exp(scores - newest_max[..., None])
    newest_sum = jnp.sum(raised, axis=-1)
    update = jnp.einsum(
        "lhqk,lkhd->lqhd",
        raised.astype(jnp.bfloat16),
        value_heads,
        preferred_element_type=jnp.float32,
    )
    weighted = update
    running_max, running_sum, weighted = (newest_max, newest_sum, weighted)
    attn_out = weighted / jnp.transpose(running_sum, (0, 2, 1))[..., None]
    log_total = running_max + jnp.log(running_sum)
    attn_low = attn_out.astype(jnp.bfloat16).reshape(tokens, model_width)
    proj_out = project(attn_low, full_projection).reshape(local_latents, block_rows, model_width)
    mid_resid = residual_in + gate_attn * proj_out
    mlp_value, mlp_pull = jax.vjp(modulated, mid_resid, shift_mlp, scale_mlp)
    mlp_input = mlp_value.astype(jnp.bfloat16).reshape(tokens, model_width)
    hidden_pre = project(mlp_input, full_expansion)
    gelu_value, gelu_pull = jax.vjp(gelu_of, hidden_pre)
    hidden_low = gelu_value.astype(jnp.bfloat16)
    mlp_out = project(hidden_low, full_contraction).reshape(local_latents, block_rows, model_width)
    block_output = mid_resid + gate_mlp * mlp_out
    teacher_gap = block_output - teacher.astype(jnp.float32)
    local_square = jnp.sum(mask_float[..., None] * teacher_gap * teacher_gap)
    square_total = lax.psum(local_square, ("dp", "seq"))
    masked_loss = square_total / (count_total * model_width)
    full_modulation, full_attention, full_projection, full_expansion, full_contraction = (
        gather_weights(low_shards)
    )
    out_grad = cotangent.astype(jnp.float32) + 2.0 * mask_float[..., None] * teacher_gap / (
        count_total * model_width
    )
    gate_mlp_grad = jnp.sum(out_grad * mlp_out, axis=1)
    mlp_out_grad = (gate_mlp * out_grad).astype(jnp.bfloat16).reshape(tokens, model_width)
    contraction_grad = left_contract(hidden_low, mlp_out_grad)
    hidden_grad = right_contract(mlp_out_grad, full_contraction)
    hidden_pre_grad = gelu_pull(hidden_grad)[0].astype(jnp.bfloat16)
    expansion_grad = left_contract(mlp_input, hidden_pre_grad)
    mlp_input_grad = right_contract(hidden_pre_grad, full_expansion).reshape(
        local_latents, block_rows, model_width
    )
    mid_part, shift_mlp_grad, scale_mlp_grad = mlp_pull(mlp_input_grad)
    mid_grad = out_grad + mid_part
    gate_attn_grad = jnp.sum(mid_grad * proj_out, axis=1)
    proj_out_grad = (gate_attn * mid_grad).astype(jnp.bfloat16).reshape(tokens, model_width)
    projection_grad = left_contract(attn_low, proj_out_grad)
    attn_out_grad = (
        right_contract(proj_out_grad, full_projection)
        .astype(jnp.bfloat16)
        .reshape(local_latents, block_rows, head_count, head_size)
    )
    delta_heads = jnp.transpose(
        jnp.sum(attn_out_grad.astype(jnp.float32) * attn_out, axis=-1), (0, 2, 1)
    )
    key_piece = lax.all_gather(key_low, "seq", axis=1, tiled=True)
    value_piece = lax.all_gather(value_low, "seq", axis=1, tiled=True)
    span = key_piece.shape[1]
    key_heads = key_piece.reshape(local_latents, span, head_count, head_size)
    value_heads = value_piece.reshape(local_latents, span, head_count, head_size)
    scores = (
        jnp.einsum("lqhd,lkhd->lhqk", query_heads, key_heads, preferred_element_type=jnp.float32)
        * score_scale
    )
    probability = jnp.exp(scores - log_total[..., None])
    value_part = jnp.einsum(
        "lhqk,lqhd->lkhd",
        probability.astype(jnp.bfloat16),
        attn_out_grad,
        preferred_element_type=jnp.float32,
    )
    prob_grad = jnp.einsum(
        "lqhd,lkhd->lhqk", attn_out_grad, value_heads, preferred_element_type=jnp.float32
    )
    score_grad = (probability * (prob_grad - delta_heads[..., None])).astype(jnp.bfloat16)
    query_grad = (
        jnp.einsum("lhqk,lkhd->lqhd", score_grad, key_heads, preferred_element_type=jnp.float32)
        * score_scale
    )
    key_part = (
        jnp.einsum("lhqk,lqhd->lkhd", score_grad, query_heads, preferred_element_type=jnp.float32)
        * score_scale
    )
    key_grad = key_part.reshape(local_latents, span, model_width)
    value_grad = value_part.reshape(local_latents, span, model_width)
    query_grad, key_grad, value_grad = (query_grad, key_grad, value_grad)
    key_own, value_own = (
        lax.psum_scatter(
            key_grad.astype(jnp.bfloat16), "seq", scatter_dimension=1, tiled=True
        ).astype(jnp.float32),
        lax.psum_scatter(
            value_grad.astype(jnp.bfloat16), "seq", scatter_dimension=1, tiled=True
        ).astype(jnp.float32),
    )
    qkv_grad = (
        jnp.concatenate(
            [query_grad.reshape(local_latents, block_rows, model_width), key_own, value_own],
            axis=-1,
        )
        .astype(jnp.bfloat16)
        .reshape(tokens, 3 * model_width)
    )
    attention_grad = left_contract(attn_input, qkv_grad)
    attn_input_grad = right_contract(qkv_grad, full_attention).reshape(
        local_latents, block_rows, model_width
    )
    resid_part, shift_attn_grad, scale_attn_grad = attn_pull(attn_input_grad)
    latent_grad = mid_grad + resid_part
    modulation_local = jnp.concatenate(
        [
            shift_attn_grad[:, 0, :],
            scale_attn_grad[:, 0, :],
            gate_attn_grad,
            shift_mlp_grad[:, 0, :],
            scale_mlp_grad[:, 0, :],
            gate_mlp_grad,
        ],
        axis=-1,
    )
    modulation_total = lax.psum(modulation_local.astype(jnp.bfloat16), "seq")
    row_owner = jnp.arange(local_latents, dtype=jnp.int32) % seq_devices == lax.axis_index("seq")
    owned_rows = jnp.where(row_owner[:, None], modulation_total, jnp.zeros_like(modulation_total))
    modulation_wgrad = left_contract(cond_active, owned_rows)
    condition_grad = silu_pull(right_contract(modulation_total, full_modulation))[0]
    weight_grads = (
        modulation_wgrad,
        attention_grad,
        projection_grad,
        expansion_grad,
        contraction_grad,
    )
    column_share = (
        lax.psum_scatter(
            weight_grads[0].astype(jnp.bfloat16), "dp", scatter_dimension=1, tiled=True
        ).astype(jnp.float32),
        lax.psum_scatter(
            weight_grads[1].astype(jnp.bfloat16), "dp", scatter_dimension=1, tiled=True
        ).astype(jnp.float32),
        lax.psum_scatter(
            weight_grads[2].astype(jnp.bfloat16), "dp", scatter_dimension=1, tiled=True
        ).astype(jnp.float32),
        lax.psum_scatter(
            weight_grads[3].astype(jnp.bfloat16), "dp", scatter_dimension=1, tiled=True
        ).astype(jnp.float32),
        lax.psum_scatter(
            weight_grads[4].astype(jnp.bfloat16), "dp", scatter_dimension=1, tiled=True
        ).astype(jnp.float32),
    )
    owned = (
        lax.psum_scatter(
            column_share[0].astype(jnp.bfloat16), "seq", scatter_dimension=0, tiled=True
        ).astype(jnp.float32),
        lax.psum_scatter(
            column_share[1].astype(jnp.bfloat16), "seq", scatter_dimension=0, tiled=True
        ).astype(jnp.float32),
        lax.psum_scatter(
            column_share[2].astype(jnp.bfloat16), "seq", scatter_dimension=0, tiled=True
        ).astype(jnp.float32),
        lax.psum_scatter(
            column_share[3].astype(jnp.bfloat16), "seq", scatter_dimension=0, tiled=True
        ).astype(jnp.float32),
        lax.psum_scatter(
            column_share[4].astype(jnp.bfloat16), "seq", scatter_dimension=0, tiled=True
        ).astype(jnp.float32),
    )
    step_rate = 0.06 / math.sqrt(local_latents * lax.axis_size("dp") * SEQ_LEN)
    moments = (
        modulation_moment,
        attention_moment,
        projection_moment,
        expansion_moment,
        contraction_moment,
    )
    averages = (
        modulation_average,
        attention_average,
        projection_average,
        expansion_average,
        contraction_average,
    )
    weight_next = []
    moment_next = []
    average_next = []
    for master, gradient, moment, average in zip(masters, owned, moments, averages):
        moment_new = 0.5 * moment + gradient
        master_new = master - step_rate * (gradient + 0.5 * moment_new)
        weight_next.append(master_new)
        moment_next.append(moment_new)
        average_next.append(0.5 * average + 0.5 * master_new)
    return (
        block_output,
        masked_loss,
        latent_grad,
        condition_grad,
        weight_next[0],
        weight_next[1],
        weight_next[2],
        weight_next[3],
        weight_next[4],
        moment_next[0],
        moment_next[1],
        moment_next[2],
        moment_next[3],
        moment_next[4],
        average_next[0],
        average_next[1],
        average_next[2],
        average_next[3],
        average_next[4],
    )


def solution(mesh):
    in_specs = (
        P("dp", "seq", None),
        P("dp", None),
        P("dp", "seq", None),
        P("dp", "seq", None),
        P("dp", "seq"),
        P("seq", "dp"),
        P("seq", "dp"),
        P("seq", "dp"),
        P("seq", "dp"),
        P("seq", "dp"),
        P("seq", "dp"),
        P("seq", "dp"),
        P("seq", "dp"),
        P("seq", "dp"),
        P("seq", "dp"),
        P("seq", "dp"),
        P("seq", "dp"),
        P("seq", "dp"),
        P("seq", "dp"),
        P("seq", "dp"),
    )
    out_specs = (
        P("dp", "seq", None),
        P(),
        P("dp", "seq", None),
        P("dp", None),
        P("seq", "dp"),
        P("seq", "dp"),
        P("seq", "dp"),
        P("seq", "dp"),
        P("seq", "dp"),
        P("seq", "dp"),
        P("seq", "dp"),
        P("seq", "dp"),
        P("seq", "dp"),
        P("seq", "dp"),
        P("seq", "dp"),
        P("seq", "dp"),
        P("seq", "dp"),
        P("seq", "dp"),
        P("seq", "dp"),
    )
    return jax.shard_map(body, mesh=mesh, in_specs=in_specs, out_specs=out_specs, check_vma=False)
```

profile of v0, /device:TPU:0, one launch (start us, length us, event | category | flops | bytes accessed | tf_op | source)
XLA Modules:
  0.0 1844.5 jit_solution(4027176629962772524)
XLA Ops:
  8.5 2.7 all-gather
  13.8 2.3 all-gather.1
  18.5 181.5 %all-gather.12.cloned.1.call-done = bf16[1152,6912]{0,1:T(8,128)(2,1)} async-done(((bf16[1152,432]{0,1:T(8,128)(2,1)}), bf16[1152,6912]{0,1:T(8,128)(2,1)}) %all-gather.12.cloned.1.call-update) | async-done | bytes 15925264 | tf_op jit(solution)/shard_map/all_gather | solution.py:62
  200.1 9.7 fusion.69
  210.5 100.1 %all-gather.14.cloned.1.call-done = bf16[1152,3456]{0,1:T(8,128)(2,1)} async-done(((bf16[1152,216]{0,1:T(8,128)(2,1)}), bf16[1152,3456]{0,1:T(8,128)(2,1)}) %all-gather.14.cloned.1.call-update) | async-done | bytes 7962640 | tf_op jit(solution)/shard_map/all_gather | solution.py:62
  310.6 8.7 fusion.17
  319.3 1.7 fusion.96
  321.9 1.9 all-gather.2
  325.0 2.5 all-gather.3
  329.5 2.4 all_gather.58
  334.0 2.8 copy.61
  336.8 7.8 all-gather.16.cloned.1.call-done
  344.6 4.3 copy.59
  348.9 13.5 multiply_reduce_fusion
  362.4 15.2 fusion
  377.6 15.6 fusion.97
  393.2 20.2 %all-gather.20.cloned.1.call-done = bf16[1152,1152]{0,1:T(8,128)(2,1)} async-done(((bf16[1152,72]{0,1:T(8,128)(2,1)}), bf16[1152,1152]{0,1:T(8,128)(2,1)}) %all-gather.20.cloned.1.call-update) | async-done | bytes 2654224 | tf_op jit(solution)/shard_map/all_gather | solution.py:62
  413.4 5.8 fusion.95
  422.3 126.8 %all-gather.22.cloned.1.call-done = bf16[1152,4608]{0,1:T(8,128)(2,1)} async-done(((bf16[1152,288]{0,1:T(8,128)(2,1)}), bf16[1152,4608]{0,1:T(8,128)(2,1)}) %all-gather.22.cloned.1.call-update) | async-done | bytes 10616848 | tf_op jit(solution)/shard_map/all_gather | solution.py:62
  549.1 12.6 fusion.84
  561.8 121.8 %all-gather.24.cloned.1.call-done = bf16[4608,1152]{0,1:T(8,128)(2,1)} async-done(((bf16[4608,72]{0,1:T(8,128)(2,1)}), bf16[4608,1152]{0,1:T(8,128)(2,1)}) %all-gather.24.cloned.1.call-update) | async-done | bytes 10616848 | tf_op jit(solution)/shard_map/all_gather | solution.py:62
  683.6 16.2 fusion.29
  699.9 38.6 %all-reduce.2 = (f32[]{:T(128)}, f32[]{:T(128)}) all-reduce(f32[]{:T(128)} %get-tuple-element.52, f32[]{:T(128)} %convert_reduce_fusion.2), channel_id=1, replica_groups=mesh['dp'=16,'seq'=2] {'dp','seq'}, use_global_device_ids=true, to_apply=%region_7.0 | all-reduce | flops 2 | bytes 16 | tf_op jit(solution)/shard_map/psum | solution.py:162
  739.2 4.5 fusion.30
  743.7 18.4 fusion.13
  762.1 9.3 fusion.31
  776.5 2.9 convolution_convert_fusion.5
  779.4 2.4 copy.64
  781.8 15.7 fusion.34
  797.6 2.8 copy.65
  800.4 3.1 multiply_reduce_fusion.1
  803.5 19.8 %multiply_convert_fusion = bf16[16,512,1024]{2,1,0:T(8,128)(2,1)} fusion(f32[16,512,1024]{2,1,0:T(8,128)} %get-tuple-element.60, f32[16,512]{1,0:T(8,128)S(1)} %bitcast.161, f32[16,512]{1,0:T(8,128)S(1)} %copy-done.25, bf16[512,16,72]{0,2,1:T(8,128)(2,1)S(1)} %bitcast.153, bf16[1024,16,72]{0,2,1:T(8,128)(2,1)S(1)} %bitcast.149), kind=kOutput, calls=%fused_computation | convolution fusion | flops 1249902592 | bytes 53936128 | tf_op jit(solution)/shard_map/lqhd,lkhd->lhqk/dot_general | solution.py:208
  823.2 10.3 multiply_convert_fusion.2
  835.2 3.2 convolution_convert_fusion.3
  838.5 1.6 copy-done.1
  840.1 12.8 multiply_convert_fusion.3
  852.9 10.2 convolution_convert_fusion.2
  864.8 12.6 convolution_convert_fusion.1
  877.5 1.6 copy-done.12
  879.1 10.9 convolution_convert_fusion
  892.4 9.9 fusion.28
  905.2 2.4 fusion.26
  910.5 4.6 psum.23
  916.0 6.8 multiply_convert_fusion.1
  922.8 51.9 %reduce-scatter.47.cloned.1.call-done = bf16[1152,72]{0,1:T(8,128)(2,1)} async-done(((bf16[1152,1152]{0,1:T(8,128)(2,1)}), bf16[1152,72]{0,1:T(8,128)(2,1)}) %reduce-scatter.47.cloned.1.call-update) | async-done | bytes 165904
  974.8 1.8 copy.70
  976.6 164.3 %reduce-scatter.45.cloned.1.call-done = bf16[1152,216]{0,1:T(8,128)(2,1)} async-done(((bf16[1152,3456]{0,1:T(8,128)(2,1)}), bf16[1152,216]{0,1:T(8,128)(2,1)}) %reduce-scatter.45.cloned.1.call-update) | async-done | bytes 497680
  1140.9 2.1 copy.68
  1143.1 185.4 %reduce-scatter.31.cloned.1.call-done = bf16[1152,288]{0,1:T(8,128)(2,1)} async-done(((bf16[1152,4608]{0,1:T(8,128)(2,1)}), bf16[1152,288]{0,1:T(8,128)(2,1)}) %reduce-scatter.31.cloned.1.call-update) | async-done | bytes 663568 | tf_op jit(solution)/shard_map/reduce_scatter | solution.py:278
  1328.5 2.3 copy.72
  1330.9 184.8 %reduce-scatter.33.cloned.1.call-done = bf16[4608,72]{0,1:T(8,128)(2,1)} async-done(((bf16[4608,1152]{0,1:T(8,128)(2,1)}), bf16[4608,72]{0,1:T(8,128)(2,1)}) %reduce-scatter.33.cloned.1.call-update) | async-done | bytes 663568 | tf_op jit(solution)/shard_map/reduce_scatter | solution.py:281
  1517.9 8.3 fusion.66
  1526.2 247.9 %reduce-scatter.29.cloned.1.call-done = bf16[1152,432]{0,1:T(8,128)(2,1)} async-done(((bf16[1152,6912]{0,1:T(8,128)(2,1)}), bf16[1152,432]{0,1:T(8,128)(2,1)}) %reduce-scatter.29.cloned.1.call-update) | async-done | bytes 995344 | tf_op jit(solution)/shard_map/reduce_scatter | solution.py:269
  1774.1 2.4 copy.66
  1776.5 3.9 add_add_fusion.2
  1780.4 3.8 reduce-scatter.41.cloned.1.call-done
  1785.2 1.9 add_multiply_fusion.5
  1787.2 9.0 reduce-scatter.39.cloned.1.call-done
  1797.4 2.5 add_multiply_fusion.4
  1799.9 8.5 reduce-scatter.43.cloned.1.call-done
  1811.2 8.6 reduce-scatter.35.cloned.1.call-done
  1819.9 2.8 add_multiply_fusion.3
  1822.7 9.3 reduce-scatter.37.cloned.1.call-done
  1833.5 3.2 add_multiply_fusion.1
  (211 shorter events, 41.7 us)
Async XLA Ops:
  7.2 192.9 %all-gather.12.cloned.1.call-start = ((), (), s32[]{:S(2)}) async-start(), calls=%async_computation.12 | async-start | bytes 16920576 | tf_op jit(solution)/shard_map/all_gather | solution.py:62
  13.7 4.1 copy-start.3
  13.7 296.9 %all-gather.14.cloned.1.call-start = ((), (), s32[]{:S(2)}) async-start(), calls=%async_computation.13 | async-start | bytes 8460288 | tf_op jit(solution)/shard_map/all_gather | solution.py:62
  16.1 184.0 %copy-start.35 = (bf16[1,1152]{1,0:T(2,128)(2,1)S(1)}, bf16[1,1152]{1,0:T(2,128)(2,1)}, u32[]{:S(2)}) copy-start(bf16[1,1152]{1,0:T(2,128)(2,1)} %param.21) | copy-start | bytes 6916
  17.7 316.2 %all-gather.18.cloned.1.call-start = ((), (), s32[]{:S(2)}) async-start(), calls=%async_computation.15 | async-start | bytes 3538944 | tf_op jit(solution)/shard_map/all_gather | solution.py:128
  18.0 292.5 %copy-start.37 = (f32[512]{0:T(512)}, f32[512]{0:T(512)S(1)}, u32[]{:S(2)}) copy-start(f32[512]{0:T(512)S(1)} %broadcast_multiply_fusion.2) | copy-start | bytes 6148
  18.5 181.6 %copy-start.42 = (f32[512]{0:T(512)}, f32[512]{0:T(512)S(1)}, u32[]{:S(2)}) copy-start(f32[512]{0:T(512)S(1)} %fusion.27) | copy-start | bytes 6148
  18.5 292.1 %copy-start.39 = (f32[512]{0:T(512)}, f32[512]{0:T(512)S(1)}, u32[]{:S(2)}) copy-start(f32[512]{0:T(512)S(1)} %fusion.74) | copy-start | bytes 6148
  210.5 100.1 %copy-start.33 = (f32[1152]{0:T(1024)}, f32[1152]{0:T(1024)S(1)}, u32[]{:S(2)}) copy-start(f32[1152]{0:T(1024)S(1)} %get-tuple-element.26) | copy-start | bytes 13828
  210.5 100.1 %copy-start.50 = (f32[1152]{0:T(1024)}, f32[1152]{0:T(1024)S(1)}, u32[]{:S(2)}) copy-start(f32[1152]{0:T(1024)S(1)} %get-tuple-element.25) | copy-start | bytes 13828
  210.5 203.0 %copy-start.51 = (f32[1152]{0:T(1024)}, f32[1152]{0:T(1024)S(1)}, u32[]{:S(2)}) copy-start(f32[1152]{0:T(1024)S(1)} %get-tuple-element.27) | copy-start | bytes 13828
  321.0 3.9 copy-start.16
  321.0 23.6 %all-gather.16.cloned.1.call-start = ((), (), s32[]{:S(2)}) async-start(), calls=%async_computation.14 | async-start | bytes 3538944 | tf_op jit(solution)/shard_map/all_gather | solution.py:129
  321.6 91.9 %all-gather.20.cloned.1.call-start = ((), (), s32[]{:S(2)}) async-start(), calls=%async_computation.16 | async-start | bytes 2820096 | tf_op jit(solution)/shard_map/all_gather | solution.py:62
  324.8 224.3 %all-gather.22.cloned.1.call-start = ((), (), s32[]{:S(2)}) async-start(), calls=%async_computation.17 | async-start | bytes 11280384 | tf_op jit(solution)/shard_map/all_gather | solution.py:62
  324.9 4.5 copy-start.18
  328.0 4.0 copy-start.54
  329.4 354.3 %all-gather.24.cloned.1.call-start = ((), (), s32[]{:S(2)}) async-start(), calls=%async_computation.18 | async-start | bytes 11280384 | tf_op jit(solution)/shard_map/all_gather | solution.py:62
  331.9 521.0 %reduce-scatter.27.cloned.1.call-start = ((), (), s32[]{:S(2)}) async-start(), calls=%async_computation.20 | async-start | bytes 3538944 | tf_op jit(solution)/shard_map/reduce_scatter | solution.py:227
  336.8 12.1 copy-start
  362.4 15.2 copy-start.29
  362.4 15.2 copy-start.32
  362.4 15.2 copy-start.2
  419.3 352.1 %copy-start.41 = (f32[512]{0:T(512)}, f32[512]{0:T(512)S(1)}, u32[]{:S(2)}) copy-start(f32[512]{0:T(512)S(1)} %broadcast_multiply_fusion.1) | copy-start | bytes 6148
  739.1 4.5 copy-start.48
  739.2 22.9 %slice-start = ((s8[10616832]{0:T(1024)(128)(4,1)}), s8[4194304]{0:T(1024)(128)(4,1)S(1)}, s32[]{:S(2)}) async-start(s8[10616832]{0:T(1024)(128)(4,1)} %bitcast.165), calls=%async_computation.31 | async-start | bytes 8388608
  743.6 29.2 %copy-start.11 = (f32[1,512,1152]{2,1,0:T(8,128)}, f32[1,512,1152]{2,1,0:T(8,128)S(1)}, u32[]{:S(2)}) copy-start(f32[1,512,1152]{2,1,0:T(8,128)S(1)} %get-tuple-element.47) | copy-start | bytes 7077892
  743.6 18.4 copy-start.9
  743.6 18.4 copy-start.47
  743.6 18.4 slice-start.1
  743.6 18.4 slice-start.2
  771.4 2.5 copy-start.20
  773.9 2.6 copy-start.52
  774.0 2.6 copy-start.57
  797.5 55.4 %reduce-scatter.25.cloned.1.call-start = ((), (), s32[]{:S(2)}) async-start(), calls=%async_computation.19 | async-start | bytes 3538944 | tf_op jit(solution)/shard_map/reduce_scatter | solution.py:224
  800.4 3.1 copy-start.5
  800.4 3.1 copy-start.25
  823.2 10.6 copy-start.23
  823.2 10.6 copy-start.53
  833.6 141.2 %reduce-scatter.47.cloned.1.call-start = ((), (), s32[]{:S(2)}) async-start(), calls=%async_computation.30 | async-start | bytes 2820096
  838.5 14.5 copy-start.4
  838.5 14.4 copy-start.34
  838.5 302.4 %reduce-scatter.45.cloned.1.call-start = ((), (), s32[]{:S(2)}) async-start(), calls=%async_computation.29 | async-start | bytes 8460288
  863.1 465.4 %reduce-scatter.31.cloned.1.call-start = ((), (), s32[]{:S(2)}) async-start(), calls=%async_computation.22 | async-start | bytes 11280384 | tf_op jit(solution)/shard_map/reduce_scatter | solution.py:278
  877.4 638.3 %reduce-scatter.33.cloned.1.call-start = ((), (), s32[]{:S(2)}) async-start(), calls=%async_computation.23 | async-start | bytes 11280384 | tf_op jit(solution)/shard_map/reduce_scatter | solution.py:281
  890.0 884.0 %reduce-scatter.29.cloned.1.call-start = ((), (), s32[]{:S(2)}) async-start(), calls=%async_computation.21 | async-start | bytes 16920576 | tf_op jit(solution)/shard_map/reduce_scatter | solution.py:269
  903.1 5.0 copy-start.45
  903.1 5.6 copy-start.46
  903.1 6.2 copy-start.56
  903.1 6.8 copy-start.44
  922.8 861.4 %reduce-scatter.41.cloned.1.call-start = ((), (), s32[]{:S(2)}) async-start(), calls=%async_computation.27 | async-start | bytes 442368
  976.6 819.6 %reduce-scatter.39.cloned.1.call-start = ((), (), s32[]{:S(2)}) async-start(), calls=%async_computation.26 | async-start | bytes 884736
  1143.0 665.4 %reduce-scatter.43.cloned.1.call-start = ((), (), s32[]{:S(2)}) async-start(), calls=%async_computation.28 | async-start | bytes 1327104
  1330.8 489.1 %reduce-scatter.35.cloned.1.call-start = ((), (), s32[]{:S(2)}) async-start(), calls=%async_computation.24 | async-start | bytes 995328 | tf_op jit(solution)/shard_map/reduce_scatter | solution.py:298
  1515.7 316.4 %reduce-scatter.37.cloned.1.call-start = ((), (), s32[]{:S(2)}) async-start(), calls=%async_computation.25 | async-start | bytes 1769472
  1526.2 250.3 %copy-start.38 = (f32[512]{0:T(512)S(1)}, f32[512]{0:T(512)}, u32[]{:S(2)}) copy-start(f32[512]{0:T(512)} %copy-done.37) | copy-start | bytes 6148
  1526.2 250.3 %copy-start.40 = (f32[512]{0:T(512)S(1)}, f32[512]{0:T(512)}, u32[]{:S(2)}) copy-start(f32[512]{0:T(512)} %copy-done.39) | copy-start | bytes 6148
  1780.4 17.0 copy-start.22
  1787.2 22.5 %copy-start.17 = (f32[576,288]{0,1:T(8,128)S(1)}, f32[576,288]{0,1:T(8,128)}, u32[]{:S(2)}) copy-start(f32[576,288]{0,1:T(8,128)} %param.28) | copy-start | bytes 1990660
  1787.2 22.5 %copy-start.26 = (f32[576,288]{0,1:T(8,128)S(1)}, f32[576,288]{0,1:T(8,128)}, u32[]{:S(2)}) copy-start(f32[576,288]{0,1:T(8,128)} %param.38) | copy-start | bytes 1990660
  1787.2 22.5 %copy-start.27 = (f32[576,288]{0,1:T(8,128)S(1)}, f32[576,288]{0,1:T(8,128)}, u32[]{:S(2)}) copy-start(f32[576,288]{0,1:T(8,128)} %param.33) | copy-start | bytes 1990660
  1809.7 10.2 copy-start.19
  1811.2 22.2 %copy-start.15 = (f32[576,432]{0,1:T(8,128)S(1)}, f32[576,432]{0,1:T(8,128)}, u32[]{:S(2)}) copy-start(f32[576,432]{0,1:T(8,128)} %param.25) | copy-start | bytes 2985988
  1811.2 22.2 %copy-start.24 = (f32[576,432]{0,1:T(8,128)S(1)}, f32[576,432]{0,1:T(8,128)}, u32[]{:S(2)}) copy-start(f32[576,432]{0,1:T(8,128)} %param.35) | copy-start | bytes 2985988
  (16 other events, 25.9 us)
Sparse Core Ops, SparseCore 0:
  13.8 186.2 all-gather.11
  203.3 107.1 all-gather.13
  321.1 9.1 all-gather.17
  332.3 12.2 all-gather.15
  347.7 65.6 all-gather.19
  416.7 132.4 all-gather.21
  551.9 131.6 all-gather.23
  797.7 10.8 reduce-scatter.26
  833.7 10.7 reduce-scatter.24
  849.5 125.2 reduce-scatter.46
  980.7 160.2 reduce-scatter.44
  1147.6 180.8 reduce-scatter.30
  1334.3 181.3 reduce-scatter.32
  1522.3 251.6 reduce-scatter.28
  1776.8 7.3 reduce-scatter.40
  1787.0 9.1 reduce-scatter.38
  1798.9 9.4 reduce-scatter.42
  1810.6 9.2 reduce-scatter.34
  1822.2 9.8 reduce-scatter.36
where the time goes:
time: 1850 us; the launch traced here: 1840 us
  waiting for transfers between devices  1430 us (77%)
  matrix products  227 us (12%)
  other arithmetic  60.3 us (3%)
  blocking collectives  55.1 us (3%)
  local copies, waits for them, and re-layouts  51 us (3%)
    all_gather x5, waiting for transfers between devices, gather_weights(): lax.all_gather(for_sending(row_full), 'dp', axis=1, tiled=True)  550 us
    reduce_scatter x1, waiting for transfers between devices, body(): lax.psum_scatter(weight_grads[0].astype(jnp.bfloat16), 'dp', scatter_dime...  248 us
    unnamed x25, waiting for transfers between devices  248 us
    reduce_scatter x1, waiting for transfers between devices, body(): lax.psum_scatter(weight_grads[3].astype(jnp.bfloat16), 'dp', scatter_dime...  185 us
    reduce_scatter x1, waiting for transfers between devices, body(): lax.psum_scatter(weight_grads[4].astype(jnp.bfloat16), 'dp', scatter_dime...  185 us
    dot_general x5, matrix products, project(): jnp.dot(first_matrix, second_matrix, preferred_element_type=jnp.float32)  53.1 us
    dot_general x5, matrix products, right_contract(): lax.dot_general(first_matrix, second_matrix, (((1,), (1,)), ((), ())), pr...  48.8 us
    psum x1, blocking collectives, body(): square_total = lax.psum(local_square, ('dp', 'seq'))  38.6 us
  transfers between devices with their start and end apart: 19, of which 16 were waited for; matrix products, arithmetic and copies ran while one was open for 13% of the time, Pallas kernels for 0%

commit v1 on v0

v1 whole, which is shorter than its diff:
```python
import math

import jax
import jax.numpy as jnp
from jax import lax
from jax.experimental import pallas as pl
from jax.experimental.pallas import tpu as pltpu
from jax.sharding import PartitionSpec as P

HEADS = 16
SEQ_LEN = 1024

epsilon = 1e-06
low = jnp.bfloat16


def silu_of(values):
    return values * jax.nn.sigmoid(values)


def gelu_of(values):
    tanh_input = 0.7978845608028654 * (values + 0.044715 * values * values * values)
    return 0.5 * values * (1.0 + jnp.tanh(tanh_input))


def modulated(values, offset, stretch):
    centered = values - jnp.mean(values, axis=-1, keepdims=True)
    variance = jnp.mean(centered * centered, axis=-1, keepdims=True)
    return centered * lax.rsqrt(variance + epsilon) * (1.0 + stretch) + offset


def dot(first, second, over):
    return lax.dot_general(first, second, (over, ((), ())), preferred_element_type=jnp.float32)


def nn(first, second):
    return dot(first, second, ((1,), (0,)))


def nt(first, second):
    return dot(first, second, ((1,), (1,)))


def tn(first, second):
    return dot(first, second, ((0,), (0,)))


def around(pieces):
    size = lax.axis_size("seq")
    got = [pieces[0]] * size
    for r in range(1, size):
        steps = [(j, (j + r) % size) for j in range(size)]
        got[(size - r) % size] = lax.ppermute(pieces[r], "seq", steps)
    return got


def in_order(got):
    size = lax.axis_size("seq")
    me = lax.axis_index("seq")
    if size == 2:
        return [jnp.where(me == 0, got[0], got[1]), jnp.where(me == 0, got[1], got[0])]
    stacked = jnp.stack(got)
    return [lax.dynamic_index_in_dim(stacked, (j - me) % size, 0, False) for j in range(size)]


def by_distance(array, axis):
    size = lax.axis_size("seq")
    me = lax.axis_index("seq")
    return [lax.dynamic_index_in_dim(array, (me + r) % size, axis, False) for r in range(size)]


def gather_tokens(own):
    return jnp.concatenate(around([own] * lax.axis_size("seq")), axis=0)


def sum_tokens(parts):
    return sum(around(parts))


def swap(array, bit):
    size = lax.axis_size("dp")
    return lax.ppermute(array, "dp", [(j, j ^ bit) for j in range(size)])


def hypercube():
    size = lax.axis_size("dp")
    return size >= 4 and size & (size - 1) == 0


def place(pieces, distances):
    size = lax.axis_size("dp")
    index = jnp.array(distances, jnp.int32) ^ lax.axis_index("dp").astype(jnp.int32)
    each = size // len(pieces)

    def kernel(index_ref, *refs):
        sources, target, arrived = refs[: len(pieces)], refs[-2], refs[-1]
        copies = []
        for n in range(size):
            copy = pltpu.make_async_copy(
                sources[n // each].at[n % each], target.at[index_ref[n]], arrived.at[n]
            )
            copy.start()
            copies.append(copy)
        for copy in copies:
            copy.wait()

    whole = (size,) + pieces[0].shape[1:]
    return pl.pallas_call(
        kernel,
        out_shape=jax.ShapeDtypeStruct(whole, pieces[0].dtype),
        in_specs=[pl.BlockSpec(memory_space=pltpu.SMEM)]
        + [pl.BlockSpec(memory_space=pl.ANY)] * len(pieces),
        out_specs=pl.BlockSpec(memory_space=pl.ANY),
        scratch_shapes=[pltpu.SemaphoreType.DMA((size,))],
        cost_estimate=pl.CostEstimate(
            flops=0, bytes_accessed=2 * math.prod(whole) * 2, transcendentals=0
        ),
    )(index, *pieces)


def gather_columns(shard, first, last):
    size = lax.axis_size("dp")
    if not hypercube():
        return lax.all_gather(shard, "dp", axis=0)
    held, distances = shard[None], [0]
    bit = size >> 1
    while bit >= 4:
        held = jnp.concatenate([held, swap(held, bit)], axis=0)
        distances = distances + [d ^ bit for d in distances]
        bit >>= 1
    by_first = swap(held, first)
    by_last = swap(held, last)
    by_both = swap(by_first, last)
    order = [d ^ step for step in (0, first, last, first | last) for d in distances]
    return place([held, by_first, by_last, by_both], order)


def sum_columns(blocks, first, last):
    size = lax.axis_size("dp")
    if not hypercube():
        return lax.psum_scatter(blocks, "dp", scatter_dimension=0, tiled=False)
    me = lax.axis_index("dp")
    shape = blocks.shape[1:]
    split = blocks.reshape((size // 4, 2, 2) + shape)

    def group(distance):
        want = (me ^ distance) & 3
        part = lax.dynamic_slice(
            split, (0, want >> 1, want & 1) + (0,) * len(shape), (size // 4, 1, 1) + shape
        )
        return part.reshape((size // 4,) + shape)

    def plus(a, b):
        return (a.astype(jnp.float32) + b.astype(jnp.float32)).astype(a.dtype)

    far = swap(group(first | last), first)
    near = swap(group(first), first)
    through = swap(plus(group(last), far), last)
    held = plus(plus(group(0), near), through)
    bit = 4
    while bit < size:
        pairs = held.reshape((held.shape[0] // 2, 2) + shape)
        mine = (me // bit) & 1
        away = lax.dynamic_index_in_dim(pairs, 1 - mine, 1, False)
        held = plus(lax.dynamic_index_in_dim(pairs, mine, 1, False), swap(away, bit))
        bit <<= 1
    return held[0]


def body(
    latents,
    condition,
    cotangent,
    teacher,
    valid_mask,
    modulation_weight,
    attention_weight,
    projection_weight,
    expansion_weight,
    contraction_weight,
    modulation_moment,
    attention_moment,
    projection_moment,
    expansion_moment,
    contraction_moment,
    modulation_average,
    attention_average,
    projection_average,
    expansion_average,
    contraction_average,
):
    local_latents, block_rows, width = latents.shape
    seq_size, dp_size = lax.axis_size("seq"), lax.axis_size("dp")
    seq_me, dp_me = lax.axis_index("seq"), lax.axis_index("dp")
    all_latents = local_latents * dp_size
    head_size = width // HEADS
    heads = HEADS // seq_size
    own_width = heads * head_size
    score_scale = head_size ** (-0.5)
    own_tokens = local_latents * block_rows
    tokens = own_tokens * seq_size
    row_share = attention_weight.shape[0]
    mod_share = modulation_weight.shape[1]
    qkv_share = attention_weight.shape[1]
    proj_share = projection_weight.shape[1]
    hidden_share = expansion_weight.shape[1]
    hidden_piece = hidden_share // seq_size

    attention_low = attention_weight.astype(low).T
    projection_low = projection_weight.astype(low).T
    small = jnp.concatenate([attention_low, projection_low], axis=0)
    half = small.shape[0] // 2
    small_a = gather_columns(small[:half], 1, 2)
    small_b = gather_columns(small[half:], 2, 1)

    expansion_low = expansion_weight.astype(low).T.reshape(seq_size, hidden_piece, row_share)
    expansion_shard = jnp.concatenate(in_order(around(by_distance(expansion_low, 0))), axis=1)
    contraction_low = contraction_weight.astype(low).reshape(
        dp_size // seq_size, seq_size, hidden_piece, proj_share
    )
    contraction_shard = jnp.concatenate(in_order(around(by_distance(contraction_low, 1))), axis=0)
    contraction_shard = contraction_shard.reshape(dp_size * hidden_piece, proj_share).T
    expansion_full = gather_columns(expansion_shard, 1, 2).reshape(dp_size * hidden_piece, width)
    contraction_full = gather_columns(contraction_shard, 2, 1).reshape(
        width, dp_size * hidden_piece
    )

    small_full = jnp.concatenate([small_a, small_b], axis=1)
    projection_full = small_full[:, qkv_share:].reshape(width, own_width)
    attention_rows = small_full[:, :qkv_share].reshape(3, seq_size, own_width, row_share)
    attention_full = jnp.concatenate(
        in_order(around(by_distance(attention_rows, 1))), axis=-1
    ).reshape(3 * own_width, width)

    mask_float = valid_mask.astype(jnp.float32)
    chunk = math.gcd(own_tokens, 128)
    counts = jnp.sum(mask_float.reshape(own_tokens // chunk, chunk), axis=1).astype(low)
    packed = lax.all_gather(
        jnp.concatenate([condition.reshape(-1), counts])[None], ("dp", "seq"), axis=0, tiled=True
    ).reshape(dp_size, seq_size, -1)
    count_total = jnp.sum(packed[:, :, local_latents * width :].astype(jnp.float32))
    every_cond = packed[:, 0, : local_latents * width].reshape(all_latents, width)
    cond_active = silu_of(every_cond.astype(jnp.float32)).astype(low)
    cond_rows = lax.dynamic_slice(
        cond_active, (0, seq_me * row_share), (all_latents, row_share)
    )
    modulation_low = modulation_weight.astype(low)
    mod_part = nn(cond_rows, modulation_low).reshape(dp_size, local_latents, mod_share)
    mod_part = lax.all_to_all(mod_part, "dp", 0, 0, tiled=True)
    modulation = sum(around([mod_part] * seq_size))
    modulation = jnp.transpose(modulation, (1, 0, 2)).reshape(local_latents, dp_size * mod_share)
    shift_attn, scale_attn, gate_attn, shift_mlp, scale_mlp, gate_mlp = [
        group[:, None, :] for group in jnp.split(modulation, 6, axis=-1)
    ]

    residual_in = latents.astype(jnp.float32)
    attn_value, attn_pull = jax.vjp(modulated, residual_in, shift_attn, scale_attn)
    attn_input = gather_tokens(attn_value.astype(low).reshape(own_tokens, width))
    qkv_low = nt(attn_input, attention_full).astype(low)

    def to_heads(array):
        array = array.reshape(seq_size, local_latents, block_rows, heads, head_size)
        return jnp.transpose(array, (1, 0, 2, 3, 4)).reshape(
            local_latents, seq_size * block_rows, heads, head_size
        )

    def from_heads(array):
        array = array.reshape(local_latents, seq_size, block_rows, own_width)
        return jnp.transpose(array, (1, 0, 2, 3)).reshape(tokens, own_width)

    query, key, value = [
        to_heads(qkv_low[:, n * own_width : (n + 1) * own_width]) for n in range(3)
    ]
    scores = (
        jnp.einsum("lqhd,lkhd->lhqk", query, key, preferred_element_type=jnp.float32) * score_scale
    )
    top = jnp.max(scores, axis=-1)
    raised = jnp.exp(scores - top[..., None])
    total = jnp.sum(raised, axis=-1)
    weighted = jnp.einsum(
        "lhqk,lkhd->lqhd", raised.astype(low), value, preferred_element_type=jnp.float32
    )
    attn_out = weighted / jnp.transpose(total, (0, 2, 1))[..., None]
    log_total = top + jnp.log(total)
    attn_low = from_heads(attn_out.astype(low))

    def by_block(array):
        return [array[r * own_tokens : (r + 1) * own_tokens] for r in range(seq_size)]

    def own_shape(array):
        return array.reshape(local_latents, block_rows, width)

    proj_out = own_shape(sum_tokens([nt(rows, projection_full) for rows in by_block(attn_low)]))
    mid_resid = residual_in + gate_attn * proj_out

    mlp_value, mlp_pull = jax.vjp(modulated, mid_resid, shift_mlp, scale_mlp)
    mlp_input = gather_tokens(mlp_value.astype(low).reshape(own_tokens, width))
    hidden_pre = nt(mlp_input, expansion_full)
    gelu_value, gelu_pull = jax.vjp(gelu_of, hidden_pre)
    hidden_low = gelu_value.astype(low)
    mlp_out = own_shape(sum_tokens([nt(rows, contraction_full) for rows in by_block(hidden_low)]))
    block_output = mid_resid + gate_mlp * mlp_out

    teacher_gap = block_output - teacher.astype(jnp.float32)
    local_square = jnp.sum(mask_float[..., None] * teacher_gap * teacher_gap)
    out_grad = cotangent.astype(jnp.float32) + 2.0 * mask_float[..., None] * teacher_gap / (
        count_total * width
    )

    gate_mlp_grad = jnp.sum(out_grad * mlp_out, axis=1)
    mlp_out_grad = gather_tokens((gate_mlp * out_grad).astype(low).reshape(own_tokens, width))
    contraction_grad = tn(mlp_out_grad, hidden_low).astype(low)
    contraction_sum = sum_columns(
        contraction_grad.reshape(dp_size, proj_share, dp_size * hidden_piece), 1, 2
    )
    hidden_grad = nn(mlp_out_grad, contraction_full)
    hidden_pre_grad = gelu_pull(hidden_grad)[0].astype(low)
    expansion_grad = tn(hidden_pre_grad, mlp_input).astype(low)
    expansion_sum = sum_columns(expansion_grad.reshape(dp_size, hidden_piece, width), 2, 1)
    mlp_input_grad = own_shape(
        sum_tokens([nn(rows, expansion_full) for rows in by_block(hidden_pre_grad)])
    )
    mid_part, shift_mlp_grad, scale_mlp_grad = mlp_pull(mlp_input_grad)
    mid_grad = out_grad + mid_part

    gate_attn_grad = jnp.sum(mid_grad * proj_out, axis=1)
    proj_out_grad = gather_tokens((gate_attn * mid_grad).astype(low).reshape(own_tokens, width))
    projection_grad = tn(proj_out_grad, attn_low).astype(low)
    attn_out_grad = to_heads(nn(proj_out_grad, projection_full).astype(low))
    delta = jnp.transpose(
        jnp.sum(attn_out_grad.astype(jnp.float32) * attn_out, axis=-1), (0, 2, 1)
    )
    scores = (
        jnp.einsum("lqhd,lkhd->lhqk", query, key, preferred_element_type=jnp.float32) * score_scale
    )
    probability = jnp.exp(scores - log_total[..., None])
    value_grad = jnp.einsum(
        "lhqk,lqhd->lkhd",
        probability.astype(low),
        attn_out_grad,
        preferred_element_type=jnp.float32,
    )
    prob_grad = jnp.einsum(
        "lqhd,lkhd->lhqk", attn_out_grad, value, preferred_element_type=jnp.float32
    )
    score_grad = (probability * (prob_grad - delta[..., None])).astype(low)
    query_grad = (
        jnp.einsum("lhqk,lkhd->lqhd", score_grad, key, preferred_element_type=jnp.float32)
        * score_scale
    )
    key_grad = (
        jnp.einsum("lhqk,lqhd->lkhd", score_grad, query, preferred_element_type=jnp.float32)
        * score_scale
    )
    qkv_grad = jnp.concatenate(
        [from_heads(grad.astype(low)) for grad in (query_grad, key_grad, value_grad)], axis=-1
    )
    attention_grad = tn(qkv_grad, attn_input).astype(low)
    attention_grad = attention_grad.reshape(3, own_width, seq_size, row_share)
    attention_grad = jnp.stack(in_order(around(by_distance(attention_grad, 2))), axis=1)
    small_grad = jnp.concatenate(
        [
            attention_grad.reshape(dp_size, qkv_share, row_share),
            projection_grad.reshape(dp_size, proj_share, row_share),
        ],
        axis=1,
    )
    small_sum = jnp.concatenate(
        [sum_columns(small_grad[:, :half], 1, 2), sum_columns(small_grad[:, half:], 2, 1)], axis=0
    ).astype(jnp.float32)
    attn_input_grad = own_shape(
        sum_tokens([nn(rows, attention_full) for rows in by_block(qkv_grad)])
    )
    resid_part, shift_attn_grad, scale_attn_grad = attn_pull(attn_input_grad)
    latent_grad = mid_grad + resid_part

    mod_grad = jnp.concatenate(
        [
            shift_attn_grad[:, 0, :],
            scale_attn_grad[:, 0, :],
            gate_attn_grad,
            shift_mlp_grad[:, 0, :],
            scale_mlp_grad[:, 0, :],
            gate_mlp_grad,
        ],
        axis=-1,
    )
    mod_grad = sum(around([mod_grad] * seq_size)).astype(low)
    mod_grad = jnp.transpose(mod_grad.reshape(local_latents, dp_size, mod_share), (1, 0, 2))
    mod_grad = lax.all_to_all(mod_grad, "dp", 0, 0, tiled=True).reshape(all_latents, mod_share)
    modulation_sum = tn(cond_rows, mod_grad)
    cond_part = nt(mod_grad, modulation_low).reshape(dp_size, local_latents * row_share)
    squares = jnp.broadcast_to(local_square, (dp_size, 128))
    back = lax.psum_scatter(
        jnp.concatenate([cond_part, squares], axis=1), "dp", scatter_dimension=0, tiled=True
    )
    back = jnp.stack(in_order(around([back] * seq_size)), axis=0)
    square_total = jnp.sum(back[:, 0, local_latents * row_share])
    masked_loss = square_total / (count_total * width)
    cond_grad = back[:, 0, : local_latents * row_share].reshape(seq_size, local_latents, row_share)
    cond_grad = jnp.transpose(cond_grad, (1, 0, 2)).reshape(local_latents, width)
    silu_pull = jax.vjp(silu_of, condition.astype(jnp.float32))[1]
    condition_grad = silu_pull(cond_grad)[0]

    expansion_sum = around(
        by_distance(expansion_sum.reshape(hidden_piece, seq_size, row_share), 1)
    )
    expansion_sum = jnp.concatenate(in_order(expansion_sum), axis=0).T
    contraction_sum = around(
        by_distance(
            contraction_sum.T.reshape(
                seq_size, dp_size // seq_size, hidden_piece, proj_share
            ),
            0,
        )
    )
    contraction_sum = jnp.stack(in_order(contraction_sum), axis=1).reshape(
        contraction_weight.shape
    )
    gradients = (
        modulation_sum,
        small_sum[:qkv_share].T,
        small_sum[qkv_share:].T,
        expansion_sum.astype(jnp.float32),
        contraction_sum.astype(jnp.float32),
    )

    step_rate = 0.06 / math.sqrt(all_latents * SEQ_LEN)
    masters = (
        modulation_weight,
        attention_weight,
        projection_weight,
        expansion_weight,
        contraction_weight,
    )
    moments = (
        modulation_moment,
        attention_moment,
        projection_moment,
        expansion_moment,
        contraction_moment,
    )
    averages = (
        modulation_average,
        attention_average,
        projection_average,
        expansion_average,
        contraction_average,
    )
    weight_next = []
    moment_next = []
    average_next = []
    for master, gradient, moment, average in zip(masters, gradients, moments, averages):
        moment_new = 0.5 * moment + gradient
        master_new = master - step_rate * (gradient + 0.5 * moment_new)
        weight_next.append(master_new)
        moment_next.append(moment_new)
        average_next.append(0.5 * average + 0.5 * master_new)
    return (
        block_output,
        masked_loss,
        latent_grad,
        condition_grad,
        *weight_next,
        *moment_next,
        *average_next,
    )


def solution(mesh):
    tokens_spec = P("dp", "seq", None)
    weight_spec = P("seq", "dp")
    in_specs = (
        tokens_spec,
        P("dp", None),
        tokens_spec,
        tokens_spec,
        P("dp", "seq"),
    ) + (weight_spec,) * 15
    out_specs = (tokens_spec, P(), tokens_spec, P("dp", None)) + (weight_spec,) * 15
    return jax.shard_map(body, mesh=mesh, in_specs=in_specs, out_specs=out_specs, check_vma=False)
```

time: 1850 us -> 1420 us (0.77)
  waiting for transfers between devices: 1430 us -> 384 us
  Pallas kernels: 0 us -> 508 us
  starting transfers between devices: 1.57 us -> 56 us
  other arithmetic: 60.3 us -> 106 us
  matrix products: 227 us -> 198 us
  blocking collectives: 55.1 us -> 74.8 us
    reduce_scatter x6 -> x0, waiting for transfers between devices: 627 us -> none  [the longest x1 248 us: body(): lax.psum_scatter(weight_grads[0].astype(jnp.bfloat16), 'dp', scatter_dime...]
    all_gather x7 -> x0, waiting for transfers between devices: 558 us -> none  [the longest x5 550 us: gather_weights(): lax.all_gather(for_sending(row_full), 'dp', axis=1, tiled=True)]
    pallas_call x0 -> x4, Pallas kernels: none -> 508 us  [place(): pl.pallas_call(kernel, out_shape=jax.ShapeDtypeStruct(whole, pieces[0].dt...]
    ppermute x0 -> x57, waiting for transfers between devices: none -> 277 us  [the longest x40 269 us: swap(): return lax.ppermute(array, 'dp', [(j, j ^ bit) for j in range(size)])]
    unnamed x25 -> x2, waiting for transfers between devices: 248 us -> 78.8 us
    unnamed x0 -> x1, blocking collectives: none -> 74.8 us
    ppermute x0 -> x57, starting transfers between devices: none -> 43.4 us  [the longest x40 41.2 us: swap(): return lax.ppermute(array, 'dp', [(j, j ^ bit) for j in range(size)])]
    psum x2 -> x0, blocking collectives: 43.2 us -> none  [the longest x1 38.6 us: body(): square_total = lax.psum(local_square, ('dp', 'seq'))]
  transfers between devices with their start and end apart: 19 -> 60, of which waited for: 16 -> 28; matrix products, arithmetic and copies ran while one was open for 13% -> 21% of each run, Pallas kernels for 0% -> 36%
where the time goes in v1:
time: 1420 us; the launch traced here: 1410 us
  Pallas kernels  508 us (36%)
  waiting for transfers between devices  384 us (27%)
  matrix products  198 us (14%)
  other arithmetic  106 us (7%)
  blocking collectives  74.8 us (5%)
  local copies, waits for them, and re-layouts  67.6 us (5%)
  starting transfers between devices  56 us (4%)
  between operations  18.3 us (1%)
    pallas_call x4, Pallas kernels, place(): pl.pallas_call(kernel, out_shape=jax.ShapeDtypeStruct(whole, pieces[0].dt...  508 us
    ppermute x40, waiting for transfers between devices, swap(): return lax.ppermute(array, 'dp', [(j, j ^ bit) for j in range(size)])  269 us
    dot_general x19, matrix products, dot(): lax.dot_general(first, second, (over, ((), ())), preferred_element_type=j...  113 us
    unnamed x2, waiting for transfers between devices  78.8 us
    unnamed x1, blocking collectives  74.8 us
    ppermute x40, starting transfers between devices, swap(): return lax.ppermute(array, 'dp', [(j, j ^ bit) for j in range(size)])  41.2 us
  transfers between devices with their start and end apart: 60, of which 28 were waited for; matrix products, arithmetic and copies ran while one was open for 21% of the time, Pallas kernels for 36%

profile of v1, /device:TPU:0, one launch (start us, length us, event | category | flops | bytes accessed | tf_op | source)
XLA Modules:
  0.0 1411.7 jit_solution(4704529427685547270)
XLA Ops:
  12.0 4.1 collective-permute-start.2
  17.2 12.4 collective-permute-done.2
  35.8 13.3 collective-permute-done.8
  58.2 78.8 %all-reduce.5.cloned.1.call-done = bf16[36992]{0:T(1024)(128)(2,1)} async-done(((bf16[36992]{0:T(1024)(128)(2,1)}), bf16[36992]{0:T(1024)(128)(2,1)}) %all-reduce.5.cloned.1.call-update) | async-done | bytes 74000
  143.6 7.7 all-to-all-start
  153.6 4.5 collective-permute-done.10.refs_2_
  158.1 17.0 %all-to-all-done = f32[16,1,432]{2,1,0:T(1,128)S(1)} async-done(((f32[16,1,432]{2,1,0:T(1,128)}), f32[16,1,432]{2,1,0:T(1,128)S(1)}, u32[]{:S(2)}, u32[]{:S(2)}) %all-to-all-start) | async-done | bytes 27680 | tf_op jit(solution)/shard_map/all_to_all | solution.py:249
  175.1 91.2 %shard_map.376 = bf16[16,144,576]{2,1,0:T(8,128)(2,1)} custom-call(s32[16]{0:T(128)} %broadcast_xor_fusion.index_ref, bf16[4,144,576]{2,1,0:T(8,128)(2,1)} %pad_maximum_fusion.22.refs_0_, bf16[4,144,576]{2,1,0:T(8,128)(2,1)} %collective-permute-done.9.refs_1_, bf16[4,144,576]{2,1,0:T(8,128)(2,1)} %collective-permute-done.10.refs_2_, ...), custom_call_target="tpu_custom_call" | custom-call | bytes 5308416 | tf_op jit(solution)/shard_map/pallas_call | solution.py:108
  266.4 91.3 %shard_map.375 = bf16[16,144,576]{2,1,0:T(8,128)(2,1)} custom-call(s32[16]{0:T(128)} %broadcast_xor_fusion.1.index_ref, bf16[4,144,576]{2,1,0:T(8,128)(2,1)} %pad_maximum_fusion.21.refs_0_, bf16[4,144,576]{2,1,0:T(8,128)(2,1)} %collective-permute-done.4.refs_1_, bf16[4,144,576]{2,1,0:T(8,128)(2,1)} %collective-permute-done.5.refs_2_, ...), custom_call_target="tpu_custom_call" | custom-call | bytes 5308416 | tf_op jit(solution)/shard_map/pallas_call | solution.py:108
  357.7 2.7 pad_maximum_fusion
  371.5 20.4 %collective-permute-done.22 = bf16[1,72,2304]{2,1,0:T(8,128)(2,1)S(1)} collective-permute-done((bf16[1,72,2304]{2,1,0:T(8,128)(2,1)S(1)}, bf16[1,72,2304]{2,1,0:T(8,128)(2,1)S(1)}, u32[]{:S(2)}, u32[]{:S(2)}) %collective-permute-start.22) | collective-permute-done | bytes 331808 | tf_op jit(solution)/shard_map/ppermute | solution.py:82
  398.1 8.1 convolution_convert_fusion.3
  406.6 13.2 multiply_reduce_fusion
  419.8 13.6 fusion
  433.4 15.4 %fusion.111 = (bf16[1,1024,8,72]{1,3,2,0:T(8,128)(2,1)S(1)}, f32[1,1024,8,72]{1,3,2,0:T(8,128)}) fusion(f32[1024,8]{0,1:T(8,128)S(1)} %bitcast.392, bf16[1024,8,72]{0,2,1:T(8,128)(2,1)S(1)} %bitcast.333, f32[8,1024,1024]{1,2,0:T(8,128)} %get-tuple-element.94, f32[8,1024]{1,0:T(8,128)S(1)} %get-tuple-element.93), kind=kOutput, calls=%fused_computation.284 | convolution fusion | flops 1234305024 | bytes 38338560 | tf_op jit(solution)/shard_map/lhqk,lkhd->lqhd/dot_general | solution.py:280
  455.9 13.1 collective-permute-done.17
  474.3 12.3 collective-permute-done.24.refs_1_
  487.5 16.0 %collective-permute-done.18.refs_1_ = bf16[4,144,1152]{2,1,0:T(8,128)(2,1)} collective-permute-done((bf16[4,144,1152]{2,1,0:T(8,128)(2,1)}, bf16[4,144,1152]{2,1,0:T(8,128)(2,1)}, u32[]{:S(2)}, u32[]{:S(2)}) %collective-permute-start.18) | collective-permute-done | bytes 1327136 | tf_op jit(solution)/shard_map/ppermute | solution.py:82
  504.6 2.8 fusion.107
  509.6 22.2 %collective-permute-done.25.refs_2_ = bf16[4,72,2304]{2,1,0:T(8,128)(2,1)S(1)} collective-permute-done((bf16[4,72,2304]{2,1,0:T(8,128)(2,1)S(1)}, bf16[4,72,2304]{2,1,0:T(8,128)(2,1)S(1)}, u32[]{:S(2)}, u32[]{:S(2)}) %collective-permute-start.25) | collective-permute-done | bytes 1327136 | tf_op jit(solution)/shard_map/ppermute | solution.py:82
  532.9 26.4 %collective-permute-done.26.refs_3_ = bf16[4,72,2304]{2,1,0:T(8,128)(2,1)} collective-permute-done((bf16[4,72,2304]{2,1,0:T(8,128)(2,1)S(1)}, bf16[4,72,2304]{2,1,0:T(8,128)(2,1)}, u32[]{:S(2)}, u32[]{:S(2)}) %collective-permute-start.26) | collective-permute-done | bytes 1327136 | tf_op jit(solution)/shard_map/ppermute | solution.py:82
  559.3 162.7 %shard_map.378 = bf16[16,72,2304]{2,1,0:T(8,128)(2,1)} custom-call(s32[16]{0:T(128)} %broadcast_xor_fusion.index_ref, bf16[4,72,2304]{2,1,0:T(8,128)(2,1)} %copy-done.33, bf16[4,72,2304]{2,1,0:T(8,128)(2,1)} %copy-done.53, bf16[4,72,2304]{2,1,0:T(8,128)(2,1)} %copy-done.54, bf16[4,72,2304]{2,1,0:T(8,128)(2,1)} %collective-permute-done.26.refs_3_), custom_call_target="tpu_custom_call" | custom-call | bytes 10616832 | tf_op jit(solution)/shard_map/pallas_call | solution.py:108
  722.0 162.9 %shard_map.377 = bf16[16,144,1152]{2,1,0:T(8,128)(2,1)} custom-call(s32[16]{0:T(128)} %broadcast_xor_fusion.1.index_ref, bf16[4,144,1152]{2,1,0:T(8,128)(2,1)} %pad_maximum_fusion.19.refs_0_, bf16[4,144,1152]{2,1,0:T(8,128)(2,1)} %collective-permute-done.18.refs_1_, bf16[4,144,1152]{2,1,0:T(8,128)(2,1)} %collective-permute-done.19.refs_2_, ...), custom_call_target="tpu_custom_call" | custom-call | bytes 10616832 | tf_op jit(solution)/shard_map/pallas_call | solution.py:108
  884.9 13.7 fusion.14
  898.6 4.6 fusion.34
  904.7 3.5 collective-permute-done.27
  908.2 8.3 fusion.30
  920.6 3.0 collective-permute-done.28
  923.6 16.1 %fusion.11 = bf16[1024,2304]{1,0:T(8,128)(2,1)S(1)} fusion(f32[1024,2304]{1,0:T(8,128)} %get-tuple-element.99, bf16[1152,2304]{1,0:T(8,128)(2,1)} %bitcast.367, bf16[512,1152]{1,0:T(8,128)(2,1)} %collective-permute-done.28, bf16[512,1152]{1,0:T(8,128)(2,1)} %fusion.59), kind=kOutput, calls=%fused_computation.18 | convolution fusion | flops 5497159680 | bytes 21823488 | tf_op jit(solution)/shard_map/dot_general | solution.py:33
  939.8 4.7 fusion.31
  944.6 8.4 convolution_convert_fusion.1
  957.4 7.9 convolution_convert_fusion
  973.2 15.2 %collective-permute-done.46 = bf16[4,144,1152]{2,1,0:T(8,128)(2,1)} collective-permute-done((bf16[4,144,1152]{2,1,0:T(8,128)(2,1)}, bf16[4,144,1152]{2,1,0:T(8,128)(2,1)}, u32[]{:S(2)}, u32[]{:S(2)}) %collective-permute-start.46) | collective-permute-done | bytes 1327136 | tf_op jit(solution)/shard_map/ppermute | solution.py:82
  988.5 3.1 fusion.23
  992.4 8.4 collective-permute-done.52
  1000.8 3.1 fusion.21
  1004.8 6.4 fusion.39
  1012.6 2.7 fusion.106
  1017.9 3.4 fusion.40
  1021.5 35.3 %collective-permute-done.47 = bf16[4,144,1152]{2,1,0:T(8,128)(2,1)} collective-permute-done((bf16[4,144,1152]{2,1,0:T(8,128)(2,1)}, bf16[4,144,1152]{2,1,0:T(8,128)(2,1)}, u32[]{:S(2)}, u32[]{:S(2)}) %collective-permute-start.47) | collective-permute-done | bytes 1327136 | tf_op jit(solution)/shard_map/ppermute | solution.py:82
  1064.4 13.0 collective-permute-done.48
  1078.4 2.7 collective-permute-start.49
  1081.1 15.8 %collective-permute-done.54 = bf16[2,72,2304]{2,1,0:T(8,128)(2,1)S(1)} collective-permute-done((bf16[2,72,2304]{2,1,0:T(8,128)(2,1)S(1)}, bf16[2,72,2304]{2,1,0:T(8,128)(2,1)S(1)}, u32[]{:S(2)}, u32[]{:S(2)}) %collective-permute-start.54) | collective-permute-done | bytes 663584 | tf_op jit(solution)/shard_map/ppermute | solution.py:82
  1102.2 15.1 %fusion.47 = bf16[8,72,1024]{2,1,0:T(8,128)(2,1)} fusion(bf16[1024,8,72]{0,2,1:T(8,128)(2,1)S(1)} %bitcast.346, f32[8,1024,1024]{1,2,0:T(8,128)} %get-tuple-element.94, f32[8,1024]{1,0:T(8,128)S(1)} %copy-done.55), kind=kOutput, calls=%fused_computation.105 | convolution fusion | flops 1233715200 | bytes 35946496 | tf_op jit(solution)/shard_map/lhqk,lqhd->lkhd/dot_general | solution.py:337
  1117.3 18.8 %multiply_convert_fusion = bf16[8,1024,1024]{1,2,0:T(8,128)(2,1)} fusion(f32[8,1024,1024]{1,2,0:T(8,128)} %get-tuple-element.94, f32[8,1024]{1,0:T(8,128)} %bitcast.393, f32[8,1024]{1,0:T(8,128)} %log_add_fusion, bf16[1024,8,72]{0,2,1:T(8,128)(2,1)S(1)} %bitcast.347, bf16[1024,8,72]{0,2,1:T(8,128)(2,1)S(1)} %bitcast.334), kind=kOutput, calls=%fused_computation | convolution fusion | flops 1249902592 | bytes 52756480 | tf_op jit(solution)/shard_map/lqhd,lkhd->lhqk/dot_general | solution.py:343
  1136.1 12.1 multiply_convert_fusion.1
  1148.2 10.0 multiply_convert_fusion.2
  1164.7 11.6 convolution_convert_fusion.2
  1176.3 8.6 reshape.503
  1184.9 6.3 fusion.42
  1191.2 10.1 constant_dynamic-slice_fusion.9
  1215.8 2.7 add_multiply_fusion.3
  1218.5 3.5 select_bitcast_fusion.1
  1231.6 4.3 fusion.112
  1245.2 4.8 all-to-all-start.1
  1250.0 3.9 add_add_fusion.2
  1253.8 10.9 all-to-all-done.1
  1267.7 74.8 %all-reduce.2 = f32[16,704]{1,0:T(8,128)S(1)} all-reduce(f32[16,704]{1,0:T(8,128)S(1)} %concatenate.96), channel_id=3, replica_groups=mesh['dp'=16,'seq'=2] {'dp'}, use_global_device_ids=true, to_apply=%region_18.19.clone | all-reduce | flops 11264 | bytes 90112
  1348.0 3.5 add_multiply_fusion.1
  1352.3 12.7 collective-permute-done.42
  1367.2 3.4 add_convert_fusion.3
  1376.7 6.4 collective-permute-done.43
  1384.3 8.9 collective-permute-done.38
  1395.6 5.5 collective-permute-done.39
  (463 shorter events, 164.3 us)
Async XLA Ops:
  7.2 129.8 %all-reduce.5.cloned.1.call-start = ((), (), s32[]{:S(2)}) async-start(), calls=%async_computation.2 | async-start | bytes 151552
  12.0 17.6 %collective-permute-start.2 = (bf16[1,144,576]{2,1,0:T(8,128)(2,1)S(1)}, bf16[1,144,576]{2,1,0:T(8,128)(2,1)S(1)}, u32[]{:S(2)}, u32[]{:S(2)}) collective-permute-start(bf16[1,144,576]{2,1,0:T(8,128)(2,1)S(1)} %get-tuple-element.89), channel_id=1, source_target_pairs={{0,16},{2,18},{4,20},{6,22},{8,24},{10,26},{12,28},{14,30},{16,0},... | collective-permute-start | bytes 497672 | tf_op jit(solution)/shard_map/ppermute | solution.py:82
  16.1 16.9 %collective-permute-start.7 = (bf16[1,144,576]{2,1,0:T(8,128)(2,1)S(1)}, bf16[1,144,576]{2,1,0:T(8,128)(2,1)}, u32[]{:S(2)}, u32[]{:S(2)}) collective-permute-start(bf16[1,144,576]{2,1,0:T(8,128)(2,1)S(1)} %get-tuple-element.90), channel_id=1, source_target_pairs={{0,16},{2,18},{4,20},{6,22},{8,24},{10,26},{12,28},{14,30},{16,0},... | collective-permute-start | bytes 497672 | tf_op jit(solution)/shard_map/ppermute | solution.py:82
  17.0 351.9 %collective-permute-start.15 = (bf16[144,576]{1,0:T(8,128)(2,1)}, bf16[144,576]{1,0:T(8,128)(2,1)}, u32[]{:S(2)}, u32[]{:S(2)}) collective-permute-start(bf16[144,576]{1,0:T(8,128)(2,1)} %dynamic-slice_bitcast_fusion.13), channel_id=1, source_target_pairs={{0,1},{1,0},{2,3},{3,2},{4,5},{5,4},{6,7},{7,6},{8,9},{9,8},{10,11... | collective-permute-start | bytes 497672 | tf_op jit(solution)/shard_map/ppermute | solution.py:53
  30.4 22.3 %collective-permute-start.3 = (bf16[2,144,576]{2,1,0:T(8,128)(2,1)}, bf16[2,144,576]{2,1,0:T(8,128)(2,1)}, u32[]{:S(2)}, u32[]{:S(2)}) collective-permute-start(bf16[2,144,576]{2,1,0:T(8,128)(2,1)} %pad_maximum_fusion.26), channel_id=1, source_target_pairs={{0,8},{2,10},{4,12},{6,14},{8,0},{10,2},{12,4},{14,6},{16,24},{18,... | collective-permute-start | bytes 995336 | tf_op jit(solution)/shard_map/ppermute | solution.py:82
  34.7 14.4 %collective-permute-start.8 = (bf16[2,144,576]{2,1,0:T(8,128)(2,1)}, bf16[2,144,576]{2,1,0:T(8,128)(2,1)}, u32[]{:S(2)}, u32[]{:S(2)}) collective-permute-start(bf16[2,144,576]{2,1,0:T(8,128)(2,1)} %pad_maximum_fusion.27), channel_id=1, source_target_pairs={{0,8},{2,10},{4,12},{6,14},{8,0},{10,2},{12,4},{14,6},{16,24},{18,... | collective-permute-start | bytes 995336 | tf_op jit(solution)/shard_map/ppermute | solution.py:82
  35.3 330.1 %copy-start.75 = (f32[512]{0:T(512)}, f32[512]{0:T(512)S(1)}, u32[]{:S(2)}) copy-start(f32[512]{0:T(512)S(1)} %broadcast_multiply_fusion.2) | copy-start | bytes 6148
  35.7 106.6 %copy-start.22 = (f32[576,432]{0,1:T(8,128)S(1)}, f32[576,432]{0,1:T(8,128)}, u32[]{:S(2)}) copy-start(f32[576,432]{0,1:T(8,128)} %param.29) | copy-start | bytes 2985988
  51.1 89.2 %collective-permute-start.9 = (bf16[4,144,576]{2,1,0:T(8,128)(2,1)}, bf16[4,144,576]{2,1,0:T(8,128)(2,1)}, u32[]{:S(2)}, u32[]{:S(2)}) collective-permute-start(bf16[4,144,576]{2,1,0:T(8,128)(2,1)} %pad_maximum_fusion.22.refs_0_), channel_id=1, source_target_pairs={{0,4},{2,6},{4,0},{6,2},{8,12},{10,14},{12,8},{14,10},{16,20},{18,... | collective-permute-start | bytes 1990664 | tf_op jit(solution)/shard_map/ppermute | solution.py:82
  54.6 87.1 %collective-permute-start.4 = (bf16[4,144,576]{2,1,0:T(8,128)(2,1)}, bf16[4,144,576]{2,1,0:T(8,128)(2,1)}, u32[]{:S(2)}, u32[]{:S(2)}) collective-permute-start(bf16[4,144,576]{2,1,0:T(8,128)(2,1)} %pad_maximum_fusion.21.refs_0_), channel_id=1, source_target_pairs={{0,2},{2,0},{4,6},{6,4},{8,10},{10,8},{12,14},{14,12},{16,18},{18,... | collective-permute-start | bytes 1990664 | tf_op jit(solution)/shard_map/ppermute | solution.py:82
  56.7 308.7 %copy-start.77 = (f32[512]{0:T(512)}, f32[512]{0:T(512)S(1)}, u32[]{:S(2)}) copy-start(f32[512]{0:T(512)S(1)} %fusion.90) | copy-start | bytes 6148
  138.1 20.0 %collective-permute-start.10 = (bf16[4,144,576]{2,1,0:T(8,128)(2,1)}, bf16[4,144,576]{2,1,0:T(8,128)(2,1)}, u32[]{:S(2)}, u32[]{:S(2)}) collective-permute-start(bf16[4,144,576]{2,1,0:T(8,128)(2,1)} %pad_maximum_fusion.22.refs_0_), channel_id=1, source_target_pairs={{0,2},{2,0},{4,6},{6,4},{8,10},{10,8},{12,14},{14,12},{16,18},{18,... | collective-permute-start | bytes 1990664 | tf_op jit(solution)/shard_map/ppermute | solution.py:82
  139.7 126.7 %collective-permute-start.5 = (bf16[4,144,576]{2,1,0:T(8,128)(2,1)}, bf16[4,144,576]{2,1,0:T(8,128)(2,1)}, u32[]{:S(2)}, u32[]{:S(2)}) collective-permute-start(bf16[4,144,576]{2,1,0:T(8,128)(2,1)} %pad_maximum_fusion.21.refs_0_), channel_id=1, source_target_pairs={{0,4},{2,6},{4,0},{6,2},{8,12},{10,14},{12,8},{14,10},{16,20},{18,... | collective-permute-start | bytes 1990664 | tf_op jit(solution)/shard_map/ppermute | solution.py:82
  140.2 34.9 %collective-permute-start.11 = (bf16[4,144,576]{2,1,0:T(8,128)(2,1)}, bf16[4,144,576]{2,1,0:T(8,128)(2,1)}, u32[]{:S(2)}, u32[]{:S(2)}) collective-permute-start(bf16[4,144,576]{2,1,0:T(8,128)(2,1)} %collective-permute-done.9.refs_1_), channel_id=1, source_target_pairs={{0,2},{2,0},{4,6},{6,4},{8,10},{10,8},{12,14},{14,12},{16,18},{18,... | collective-permute-start | bytes 1990664 | tf_op jit(solution)/shard_map/ppermute | solution.py:82
  141.7 124.7 %collective-permute-start.6 = (bf16[4,144,576]{2,1,0:T(8,128)(2,1)}, bf16[4,144,576]{2,1,0:T(8,128)(2,1)}, u32[]{:S(2)}, u32[]{:S(2)}) collective-permute-start(bf16[4,144,576]{2,1,0:T(8,128)(2,1)} %collective-permute-done.4.refs_1_), channel_id=1, source_target_pairs={{0,4},{2,6},{4,0},{6,2},{8,12},{10,14},{12,8},{14,10},{16,20},{18,... | collective-permute-start | bytes 1990664 | tf_op jit(solution)/shard_map/ppermute | solution.py:82
  143.6 31.5 %all-to-all-start = ((f32[16,1,432]{2,1,0:T(1,128)}), f32[16,1,432]{2,1,0:T(1,128)S(1)}, u32[]{:S(2)}, u32[]{:S(2)}) async-start(f32[16,1,432]{2,1,0:T(1,128)} %copy.201), calls=%async_computation | async-start | bytes 65536 | tf_op jit(solution)/shard_map/all_to_all | solution.py:249
  158.1 208.8 %collective-permute-start.21 = (bf16[8,144,72]{2,1,0:T(8,128)(2,1)S(1)}, bf16[8,144,72]{2,1,0:T(8,128)(2,1)S(1)}, u32[]{:S(2)}, u32[]{:S(2)}) collective-permute-start(bf16[8,144,72]{2,1,0:T(8,128)(2,1)S(1)} %bitcast.397), channel_id=1, source_target_pairs={{0,1},{1,0},{2,3},{3,2},{4,5},{5,4},{6,7},{7,6},{8,9},{9,8},{10,11... | collective-permute-start | bytes 497672 | tf_op jit(solution)/shard_map/ppermute | solution.py:53
  175.1 189.4 %collective-permute-start = (f32[16,1,432]{2,1,0:T(1,128)S(1)}, f32[16,1,432]{2,1,0:T(1,128)S(1)}, u32[]{:S(2)}, u32[]{:S(2)}) collective-permute-start(f32[16,1,432]{2,1,0:T(1,128)S(1)} %all-to-all-done), channel_id=1, source_target_pairs={{0,1},{1,0},{2,3},{3,2},{4,5},{5,4},{6,7},{7,6},{8,9},{9,8},{10,11... | collective-permute-start | bytes 82952 | tf_op jit(solution)/shard_map/ppermute | solution.py:53
  364.0 30.3 %collective-permute-start.12 = (bf16[3,576,576]{2,1,0:T(8,128)(2,1)}, bf16[3,576,576]{2,1,0:T(8,128)(2,1)}, u32[]{:S(2)}, u32[]{:S(2)}) collective-permute-start(bf16[3,576,576]{2,1,0:T(8,128)(2,1)} %dynamic-slice_bitcast_fusion), channel_id=1, source_target_pairs={{0,1},{1,0},{2,3},{3,2},{4,5},{5,4},{6,7},{7,6},{8,9},{9,8},{10,11... | collective-permute-start | bytes 5971976 | tf_op jit(solution)/shard_map/ppermute | solution.py:53
  366.9 31.2 %collective-permute-start.1 = (bf16[512,1152]{1,0:T(8,128)(2,1)}, bf16[512,1152]{1,0:T(8,128)(2,1)}, u32[]{:S(2)}, u32[]{:S(2)}) collective-permute-start(bf16[512,1152]{1,0:T(8,128)(2,1)} %fusion.61), channel_id=1, source_target_pairs={{0,1},{1,0},{2,3},{3,2},{4,5},{5,4},{6,7},{7,6},{8,9},{9,8},{10,11... | collective-permute-start | bytes 3538952 | tf_op jit(solution)/shard_map/ppermute | solution.py:53
  367.3 24.5 %collective-permute-start.22 = (bf16[1,72,2304]{2,1,0:T(8,128)(2,1)S(1)}, bf16[1,72,2304]{2,1,0:T(8,128)(2,1)S(1)}, u32[]{:S(2)}, u32[]{:S(2)}) collective-permute-start(bf16[1,72,2304]{2,1,0:T(8,128)(2,1)S(1)} %bitcast.381), channel_id=1, source_target_pairs={{0,16},{2,18},{4,20},{6,22},{8,24},{10,26},{12,28},{14,30},{16,0},... | collective-permute-start | bytes 995336 | tf_op jit(solution)/shard_map/ppermute | solution.py:82
  370.0 80.3 %collective-permute-start.16 = (bf16[1,144,1152]{2,1,0:T(8,128)(2,1)S(1)}, bf16[1,144,1152]{2,1,0:T(8,128)(2,1)}, u32[]{:S(2)}, u32[]{:S(2)}) collective-permute-start(bf16[1,144,1152]{2,1,0:T(8,128)(2,1)S(1)} %maximum_bitcast_fusion), channel_id=1, source_target_pairs={{0,16},{2,18},{4,20},{6,22},{8,24},{10,26},{12,28},{14,30},{16,0},... | collective-permute-start | bytes 995336 | tf_op jit(solution)/shard_map/ppermute | solution.py:82
  392.7 60.6 %collective-permute-start.23 = (bf16[2,72,2304]{2,1,0:T(8,128)(2,1)}, bf16[2,72,2304]{2,1,0:T(8,128)(2,1)}, u32[]{:S(2)}, u32[]{:S(2)}) collective-permute-start(bf16[2,72,2304]{2,1,0:T(8,128)(2,1)} %pad_maximum_fusion.24), channel_id=1, source_target_pairs={{0,8},{2,10},{4,12},{6,14},{8,0},{10,2},{12,4},{14,6},{16,24},{18,... | collective-permute-start | bytes 1990664 | tf_op jit(solution)/shard_map/ppermute | solution.py:82
  450.1 54.5 %collective-permute-start.13 = (f32[512,1152]{1,0:T(8,128)S(1)}, f32[512,1152]{1,0:T(8,128)S(1)}, u32[]{:S(2)}, u32[]{:S(2)}) collective-permute-start(f32[512,1152]{1,0:T(8,128)S(1)} %fusion.113), channel_id=1, source_target_pairs={{0,1},{1,0},{2,3},{3,2},{4,5},{5,4},{6,7},{7,6},{8,9},{9,8},{10,11... | collective-permute-start | bytes 7077896 | tf_op jit(solution)/shard_map/ppermute | solution.py:53
  451.3 17.6 %collective-permute-start.17 = (bf16[2,144,1152]{2,1,0:T(8,128)(2,1)S(1)}, bf16[2,144,1152]{2,1,0:T(8,128)(2,1)S(1)}, u32[]{:S(2)}, u32[]{:S(2)}) collective-permute-start(bf16[2,144,1152]{2,1,0:T(8,128)(2,1)S(1)} %pad_maximum_fusion.23), channel_id=1, source_target_pairs={{0,8},{2,10},{4,12},{6,14},{8,0},{10,2},{12,4},{14,6},{16,24},{18,... | collective-permute-start | bytes 1990664 | tf_op jit(solution)/shard_map/ppermute | solution.py:82
  454.6 32.0 %collective-permute-start.24 = (bf16[4,72,2304]{2,1,0:T(8,128)(2,1)S(1)}, bf16[4,72,2304]{2,1,0:T(8,128)(2,1)S(1)}, u32[]{:S(2)}, u32[]{:S(2)}) collective-permute-start(bf16[4,72,2304]{2,1,0:T(8,128)(2,1)S(1)} %pad_maximum_fusion.20.refs_0_), channel_id=1, source_target_pairs={{0,4},{2,6},{4,0},{6,2},{8,12},{10,14},{12,8},{14,10},{16,20},{18,... | collective-permute-start | bytes 3981320 | tf_op jit(solution)/shard_map/ppermute | solution.py:82
  471.1 32.3 %collective-permute-start.18 = (bf16[4,144,1152]{2,1,0:T(8,128)(2,1)}, bf16[4,144,1152]{2,1,0:T(8,128)(2,1)}, u32[]{:S(2)}, u32[]{:S(2)}) collective-permute-start(bf16[4,144,1152]{2,1,0:T(8,128)(2,1)} %pad_maximum_fusion.19.refs_0_), channel_id=1, source_target_pairs={{0,2},{2,0},{4,6},{6,4},{8,10},{10,8},{12,14},{14,12},{16,18},{18,... | collective-permute-start | bytes 3981320 | tf_op jit(solution)/shard_map/ppermute | solution.py:82
  472.0 59.8 %collective-permute-start.25 = (bf16[4,72,2304]{2,1,0:T(8,128)(2,1)S(1)}, bf16[4,72,2304]{2,1,0:T(8,128)(2,1)S(1)}, u32[]{:S(2)}, u32[]{:S(2)}) collective-permute-start(bf16[4,72,2304]{2,1,0:T(8,128)(2,1)S(1)} %pad_maximum_fusion.20.refs_0_), channel_id=1, source_target_pairs={{0,2},{2,0},{4,6},{6,4},{8,10},{10,8},{12,14},{14,12},{16,18},{18,... | collective-permute-start | bytes 3981320 | tf_op jit(solution)/shard_map/ppermute | solution.py:82
  473.2 248.8 %collective-permute-start.19 = (bf16[4,144,1152]{2,1,0:T(8,128)(2,1)}, bf16[4,144,1152]{2,1,0:T(8,128)(2,1)}, u32[]{:S(2)}, u32[]{:S(2)}) collective-permute-start(bf16[4,144,1152]{2,1,0:T(8,128)(2,1)} %pad_maximum_fusion.19.refs_0_), channel_id=1, source_target_pairs={{0,4},{2,6},{4,0},{6,2},{8,12},{10,14},{12,8},{14,10},{16,20},{18,... | collective-permute-start | bytes 3981320 | tf_op jit(solution)/shard_map/ppermute | solution.py:82
  486.6 72.6 %collective-permute-start.26 = (bf16[4,72,2304]{2,1,0:T(8,128)(2,1)S(1)}, bf16[4,72,2304]{2,1,0:T(8,128)(2,1)}, u32[]{:S(2)}, u32[]{:S(2)}) collective-permute-start(bf16[4,72,2304]{2,1,0:T(8,128)(2,1)S(1)} %collective-permute-done.24.refs_1_), channel_id=1, source_target_pairs={{0,2},{2,0},{4,6},{6,4},{8,10},{10,8},{12,14},{14,12},{16,18},{18,... | collective-permute-start | bytes 3981320 | tf_op jit(solution)/shard_map/ppermute | solution.py:82
  503.4 218.6 %collective-permute-start.20 = (bf16[4,144,1152]{2,1,0:T(8,128)(2,1)}, bf16[4,144,1152]{2,1,0:T(8,128)(2,1)}, u32[]{:S(2)}, u32[]{:S(2)}) collective-permute-start(bf16[4,144,1152]{2,1,0:T(8,128)(2,1)} %collective-permute-done.18.refs_1_), channel_id=1, source_target_pairs={{0,4},{2,6},{4,0},{6,2},{8,12},{10,14},{12,8},{14,10},{16,20},{18,... | collective-permute-start | bytes 3981320 | tf_op jit(solution)/shard_map/ppermute | solution.py:82
  509.6 375.3 %collective-permute-start.14 = (bf16[512,1152]{1,0:T(8,128)(2,1)}, bf16[512,1152]{1,0:T(8,128)(2,1)}, u32[]{:S(2)}, u32[]{:S(2)}) collective-permute-start(bf16[512,1152]{1,0:T(8,128)(2,1)} %fusion.58), channel_id=1, source_target_pairs={{0,1},{1,0},{2,3},{3,2},{4,5},{5,4},{6,7},{7,6},{8,9},{9,8},{10,11... | collective-permute-start | bytes 3538952 | tf_op jit(solution)/shard_map/ppermute | solution.py:53
  722.0 176.6 %slice-start.4 = ((s8[5308416]{0:T(1024)(128)(4,1)}), s8[1114112]{0:T(1024)(128)(4,1)S(1)}, s32[]{:S(2)}) async-start(s8[5308416]{0:T(1024)(128)(4,1)} %bitcast.368), calls=%async_computation.7 | async-start | bytes 2228224
  903.3 4.9 collective-permute-start.27
  920.5 3.2 collective-permute-start.28
  944.5 60.3 %collective-permute-start.29 = (f32[512,1152]{1,0:T(8,128)}, f32[512,1152]{1,0:T(8,128)}, u32[]{:S(2)}, u32[]{:S(2)}) collective-permute-start(f32[512,1152]{1,0:T(8,128)} %fusion.31), channel_id=1, source_target_pairs={{0,1},{1,0},{2,3},{3,2},{4,5},{5,4},{6,7},{7,6},{8,9},{9,8},{10,11... | collective-permute-start | bytes 7077896 | tf_op jit(solution)/shard_map/ppermute | solution.py:53
  956.2 32.3 %collective-permute-start.46 = (bf16[4,144,1152]{2,1,0:T(8,128)(2,1)}, bf16[4,144,1152]{2,1,0:T(8,128)(2,1)}, u32[]{:S(2)}, u32[]{:S(2)}) collective-permute-start(bf16[4,144,1152]{2,1,0:T(8,128)(2,1)} %get-tuple-element.61), channel_id=1, source_target_pairs={{0,4},{2,6},{4,0},{6,2},{8,12},{10,14},{12,8},{14,10},{16,20},{18,... | collective-permute-start | bytes 3981320 | tf_op jit(solution)/shard_map/ppermute | solution.py:82
  968.5 32.3 %collective-permute-start.52 = (bf16[4,72,2304]{2,1,0:T(8,128)(2,1)}, bf16[4,72,2304]{2,1,0:T(8,128)(2,1)}, u32[]{:S(2)}, u32[]{:S(2)}) collective-permute-start(bf16[4,72,2304]{2,1,0:T(8,128)(2,1)} %get-tuple-element.59), channel_id=1, source_target_pairs={{0,2},{2,0},{4,6},{6,4},{8,10},{10,8},{12,14},{14,12},{16,18},{18,... | collective-permute-start | bytes 3981320 | tf_op jit(solution)/shard_map/ppermute | solution.py:82
  971.2 50.3 %collective-permute-start.45 = (bf16[4,144,1152]{2,1,0:T(8,128)(2,1)}, bf16[4,144,1152]{2,1,0:T(8,128)(2,1)}, u32[]{:S(2)}, u32[]{:S(2)}) collective-permute-start(bf16[4,144,1152]{2,1,0:T(8,128)(2,1)} %get-tuple-element.60), channel_id=1, source_target_pairs={{0,4},{2,6},{4,0},{6,2},{8,12},{10,14},{12,8},{14,10},{16,20},{18,... | collective-permute-start | bytes 3981320 | tf_op jit(solution)/shard_map/ppermute | solution.py:82
  972.0 89.1 %collective-permute-start.51 = (bf16[4,72,2304]{2,1,0:T(8,128)(2,1)}, bf16[4,72,2304]{2,1,0:T(8,128)(2,1)}, u32[]{:S(2)}, u32[]{:S(2)}) collective-permute-start(bf16[4,72,2304]{2,1,0:T(8,128)(2,1)} %get-tuple-element.58), channel_id=1, source_target_pairs={{0,2},{2,0},{4,6},{6,4},{8,10},{10,8},{12,14},{14,12},{16,18},{18,... | collective-permute-start | bytes 3981320 | tf_op jit(solution)/shard_map/ppermute | solution.py:82
  991.6 65.2 %collective-permute-start.47 = (bf16[4,144,1152]{2,1,0:T(8,128)(2,1)}, bf16[4,144,1152]{2,1,0:T(8,128)(2,1)}, u32[]{:S(2)}, u32[]{:S(2)}) collective-permute-start(bf16[4,144,1152]{2,1,0:T(8,128)(2,1)} %fusion.23), channel_id=1, source_target_pairs={{0,2},{2,0},{4,6},{6,4},{8,10},{10,8},{12,14},{14,12},{16,18},{18,... | collective-permute-start | bytes 3981320 | tf_op jit(solution)/shard_map/ppermute | solution.py:82
  1003.9 57.2 %collective-permute-start.53 = (bf16[4,72,2304]{2,1,0:T(8,128)(2,1)}, bf16[4,72,2304]{2,1,0:T(8,128)(2,1)}, u32[]{:S(2)}, u32[]{:S(2)}) collective-permute-start(bf16[4,72,2304]{2,1,0:T(8,128)(2,1)} %fusion.21), channel_id=1, source_target_pairs={{0,4},{2,6},{4,0},{6,2},{8,12},{10,14},{12,8},{14,10},{16,20},{18,... | collective-permute-start | bytes 3981320 | tf_op jit(solution)/shard_map/ppermute | solution.py:82
  1021.4 77.9 %collective-permute-start.30 = (bf16[512,1152]{1,0:T(8,128)(2,1)S(1)}, bf16[512,1152]{1,0:T(8,128)(2,1)S(1)}, u32[]{:S(2)}, u32[]{:S(2)}) collective-permute-start(bf16[512,1152]{1,0:T(8,128)(2,1)S(1)} %fusion.60), channel_id=1, source_target_pairs={{0,1},{1,0},{2,3},{3,2},{4,5},{5,4},{6,7},{7,6},{8,9},{9,8},{10,11... | collective-permute-start | bytes 3538952 | tf_op jit(solution)/shard_map/ppermute | solution.py:53
  1059.5 17.9 %collective-permute-start.48 = (bf16[2,144,1152]{2,1,0:T(8,128)(2,1)S(1)}, bf16[2,144,1152]{2,1,0:T(8,128)(2,1)S(1)}, u32[]{:S(2)}, u32[]{:S(2)}) collective-permute-start(bf16[2,144,1152]{2,1,0:T(8,128)(2,1)S(1)} %dynamic-slice_bitcast_fusion.10), channel_id=1, source_target_pairs={{0,8},{2,10},{4,12},{6,14},{8,0},{10,2},{12,4},{14,6},{16,24},{18,... | collective-permute-start | bytes 1990664 | tf_op jit(solution)/shard_map/ppermute | solution.py:82
  1063.8 33.1 %collective-permute-start.54 = (bf16[2,72,2304]{2,1,0:T(8,128)(2,1)S(1)}, bf16[2,72,2304]{2,1,0:T(8,128)(2,1)S(1)}, u32[]{:S(2)}, u32[]{:S(2)}) collective-permute-start(bf16[2,72,2304]{2,1,0:T(8,128)(2,1)S(1)} %dynamic-slice_bitcast_fusion.9), channel_id=1, source_target_pairs={{0,8},{2,10},{4,12},{6,14},{8,0},{10,2},{12,4},{14,6},{16,24},{18,... | collective-permute-start | bytes 1990664 | tf_op jit(solution)/shard_map/ppermute | solution.py:82
  1078.4 125.0 %collective-permute-start.49 = (bf16[1,144,1152]{2,1,0:T(8,128)(2,1)}, bf16[1,144,1152]{2,1,0:T(8,128)(2,1)}, u32[]{:S(2)}, u32[]{:S(2)}) collective-permute-start(bf16[1,144,1152]{2,1,0:T(8,128)(2,1)} %constant_dynamic-slice_fusion.5), channel_id=1, source_target_pairs={{0,16},{2,18},{4,20},{6,22},{8,24},{10,26},{12,28},{14,30},{16,0},... | collective-permute-start | bytes 995336 | tf_op jit(solution)/shard_map/ppermute | solution.py:82
  1098.6 107.2 %collective-permute-start.55 = (bf16[1,72,2304]{2,1,0:T(8,128)(2,1)}, bf16[1,72,2304]{2,1,0:T(8,128)(2,1)}, u32[]{:S(2)}, u32[]{:S(2)}) collective-permute-start(bf16[1,72,2304]{2,1,0:T(8,128)(2,1)} %constant_dynamic-slice_fusion.2), channel_id=1, source_target_pairs={{0,16},{2,18},{4,20},{6,22},{8,24},{10,26},{12,28},{14,30},{16,0},... | collective-permute-start | bytes 995336 | tf_op jit(solution)/shard_map/ppermute | solution.py:82
  1191.2 40.4 %collective-permute-start.31 = (f32[512,1152]{1,0:T(8,128)}, f32[512,1152]{1,0:T(8,128)}, u32[]{:S(2)}, u32[]{:S(2)}) collective-permute-start(f32[512,1152]{1,0:T(8,128)} %fusion.42), channel_id=1, source_target_pairs={{0,1},{1,0},{2,3},{3,2},{4,5},{5,4},{6,7},{7,6},{8,9},{9,8},{10,11... | collective-permute-start | bytes 7077896 | tf_op jit(solution)/shard_map/ppermute | solution.py:53
  1203.0 15.6 %collective-permute-start.34 = (bf16[3,576,576]{2,1,0:T(8,128)(2,1)}, bf16[3,576,576]{2,1,0:T(8,128)(2,1)}, u32[]{:S(2)}, u32[]{:S(2)}) collective-permute-start(bf16[3,576,576]{2,1,0:T(8,128)(2,1)} %bitcast.324), channel_id=1, source_target_pairs={{0,1},{1,0},{2,3},{3,2},{4,5},{5,4},{6,7},{7,6},{8,9},{9,8},{10,11... | collective-permute-start | bytes 5971976 | tf_op jit(solution)/shard_map/ppermute | solution.py:53
  1205.7 3.3 collective-permute-start.50
  1208.6 1.7 collective-permute-start.56
  1226.2 126.1 %collective-permute-start.40 = (bf16[4,144,576]{2,1,0:T(8,128)(2,1)}, bf16[4,144,576]{2,1,0:T(8,128)(2,1)}, u32[]{:S(2)}, u32[]{:S(2)}) collective-permute-start(bf16[4,144,576]{2,1,0:T(8,128)(2,1)} %get-tuple-element.71), channel_id=1, source_target_pairs={{0,4},{2,6},{4,0},{6,2},{8,12},{10,14},{12,8},{14,10},{16,20},{18,... | collective-permute-start | bytes 1990664 | tf_op jit(solution)/shard_map/ppermute | solution.py:82
  1227.2 116.0 %collective-permute-start.41 = (bf16[4,144,576]{2,1,0:T(8,128)(2,1)}, bf16[4,144,576]{2,1,0:T(8,128)(2,1)}, u32[]{:S(2)}, u32[]{:S(2)}) collective-permute-start(bf16[4,144,576]{2,1,0:T(8,128)(2,1)} %get-tuple-element.72), channel_id=1, source_target_pairs={{0,4},{2,6},{4,0},{6,2},{8,12},{10,14},{12,8},{14,10},{16,20},{18,... | collective-permute-start | bytes 1990664 | tf_op jit(solution)/shard_map/ppermute | solution.py:82
  1229.5 122.8 %collective-permute-start.35 = (bf16[4,144,576]{2,1,0:T(8,128)(2,1)}, bf16[4,144,576]{2,1,0:T(8,128)(2,1)}, u32[]{:S(2)}, u32[]{:S(2)}) collective-permute-start(bf16[4,144,576]{2,1,0:T(8,128)(2,1)} %get-tuple-element.69), channel_id=1, source_target_pairs={{0,2},{2,0},{4,6},{6,4},{8,10},{10,8},{12,14},{14,12},{16,18},{18,... | collective-permute-start | bytes 1990664 | tf_op jit(solution)/shard_map/ppermute | solution.py:82
  1230.6 115.2 %collective-permute-start.36 = (bf16[4,144,576]{2,1,0:T(8,128)(2,1)}, bf16[4,144,576]{2,1,0:T(8,128)(2,1)}, u32[]{:S(2)}, u32[]{:S(2)}) collective-permute-start(bf16[4,144,576]{2,1,0:T(8,128)(2,1)} %get-tuple-element.70), channel_id=1, source_target_pairs={{0,2},{2,0},{4,6},{6,4},{8,10},{10,8},{12,14},{14,12},{16,18},{18,... | collective-permute-start | bytes 1990664 | tf_op jit(solution)/shard_map/ppermute | solution.py:82
  1237.8 1.3 collective-permute-start.32
  1245.2 19.6 %all-to-all-start.1 = ((bf16[16,2,216]{2,1,0:T(2,128)(2,1)}), bf16[16,2,216]{2,1,0:T(2,128)(2,1)}, u32[]{:S(2)}, u32[]{:S(2)}) async-start(bf16[16,2,216]{2,1,0:T(2,128)(2,1)} %reshape.550), calls=%async_computation.1 | async-start | bytes 32768 | tf_op jit(solution)/shard_map/all_to_all | solution.py:390
  1343.2 8.3 collective-permute-start.33
  1345.8 19.2 %collective-permute-start.42 = (bf16[4,144,576]{2,1,0:T(8,128)(2,1)}, bf16[4,144,576]{2,1,0:T(8,128)(2,1)}, u32[]{:S(2)}, u32[]{:S(2)}) collective-permute-start(bf16[4,144,576]{2,1,0:T(8,128)(2,1)} %fusion.52), channel_id=1, source_target_pairs={{0,2},{2,0},{4,6},{6,4},{8,10},{10,8},{12,14},{14,12},{16,18},{18,... | collective-permute-start | bytes 1990664 | tf_op jit(solution)/shard_map/ppermute | solution.py:82
  1348.0 19.2 %collective-permute-start.37 = (bf16[4,144,576]{2,1,0:T(8,128)(2,1)}, bf16[4,144,576]{2,1,0:T(8,128)(2,1)}, u32[]{:S(2)}, u32[]{:S(2)}) collective-permute-start(bf16[4,144,576]{2,1,0:T(8,128)(2,1)} %fusion.54), channel_id=1, source_target_pairs={{0,4},{2,6},{4,0},{6,2},{8,12},{10,14},{12,8},{14,10},{16,20},{18,... | collective-permute-start | bytes 1990664 | tf_op jit(solution)/shard_map/ppermute | solution.py:82
  1371.5 11.6 collective-permute-start.43
  1374.6 18.6 %collective-permute-start.38 = (bf16[2,144,576]{2,1,0:T(8,128)(2,1)S(1)}, bf16[2,144,576]{2,1,0:T(8,128)(2,1)S(1)}, u32[]{:S(2)}, u32[]{:S(2)}) collective-permute-start(bf16[2,144,576]{2,1,0:T(8,128)(2,1)S(1)} %dynamic-slice_bitcast_fusion.12), channel_id=1, source_target_pairs={{0,8},{2,10},{4,12},{6,14},{8,0},{10,2},{12,4},{14,6},{16,24},{18,... | collective-permute-start | bytes 995336 | tf_op jit(solution)/shard_map/ppermute | solution.py:82
  1384.2 11.3 collective-permute-start.44
  1393.3 7.8 collective-permute-start.39
  (109 other events, 1454.1 us)
Sparse Core Ops, SparseCore 0:
  14.2 122.7 all-reduce.4
